TPU v7x, 32 devices: a whole 2x2x4 slice. The times are simulated.
32 devices in a mesh: blk: 4 (over y, x), fsdp: 8 (over z, core).
Axes of the slice: x: 2, y: 2, z: 4, core: 2. Of those that a mesh axis runs over, the one named last changes fastest.
Arguments:
- tokens: bfloat16 [4, 4096, 2048], P('blk', 'fsdp'), may hold values from -21 to 21
- student_weight: float32 [4, 2560, 2048], P('blk', 'fsdp'), may hold values from -0.125 to 0.125
- snapshot: bfloat16 [4, 2560, 2048], P('blk', 'fsdp'), may hold values from -0.125 to 0.125
- moment_one: float32 [4, 2560, 2048], P('blk', 'fsdp'), may hold values from -0.6 to 0.6
- moment_two: float32 [4, 2560, 2048], P('blk', 'fsdp'), may hold values from 0.001 to 0.1
Outputs:
- new_weight: float32 [4, 2560, 2048], P('blk', 'fsdp')
- new_moment_one: float32 [4, 2560, 2048], P('blk', 'fsdp')
- new_moment_two: float32 [4, 2560, 2048], P('blk', 'fsdp')
All inputs are finite; a program needn't handle non-finite values.
Results may differ from a plain program's by a relative error of at most 0.0045.
The roundings to bfloat16 on the way count: a program that leaves them out, or rounds other values in their place, can miss the bound.
Values may be sent and summed in bfloat16 or wider, within the bound.
A program may use at most 128 MiB of HBM per device.

v0:
```python
import math

import jax
import jax.numpy as jnp
from jax import lax
from jax.sharding import PartitionSpec as P

HEADS = 16
KVH = 4
HD = 128
SEQ = 256
STEP = 100


THETA = 500000.0
BETA_ONE = 0.9
BETA_TWO = 0.95
LEARN_RATE = 0.002
DECAY = 0.1
EPSILON = 1e-08
MASKED = -1e30


def shifted(value, axis, steps):
    count = lax.axis_size(axis)
    pairs = [(source, (source + steps) % count) for source in range(count)]
    return lax.ppermute(value, axis, pairs)


def rotary_tables(row_count, seq_len, head_size):
    positions = (jnp.arange(row_count) % seq_len).astype(jnp.float32)
    exponents = jnp.arange(head_size // 2).astype(jnp.float32) * (2.0 / head_size)
    frequency = THETA ** (-exponents)
    angles = positions[:, None] * frequency[None, :]
    return (jnp.cos(angles)[:, None, :], jnp.sin(angles)[:, None, :])


def rotate(vectors, cosine, sine_table, direction):
    row_count = vectors.shape[0]
    shaped = vectors.reshape(row_count, -1, HD)
    half_size = HD // 2
    front_half = shaped[..., :half_size]
    back_half = shaped[..., half_size:]
    turned = jnp.concatenate(
        [
            front_half * cosine - direction * back_half * sine_table,
            back_half * cosine + direction * front_half * sine_table,
        ],
        axis=-1,
    )
    return turned.reshape(row_count, -1)


def score_gradient(qk_student, qk_teacher):
    row_count = qk_student.shape[0]
    seq_count = row_count // SEQ
    group_size = HEADS // KVH
    inv_root = 1.0 / math.sqrt(HD)
    causal = jnp.arange(SEQ)[:, None] >= jnp.arange(SEQ)[None, :]

    def split_heads(packed):
        queries = packed[:, : HEADS * HD].reshape(seq_count, SEQ, KVH, group_size, HD)
        key_rows = packed[:, HEADS * HD :].reshape(seq_count, SEQ, KVH, HD)
        return (queries, key_rows)

    def log_probs(queries, key_rows):
        scores = (
            jnp.einsum("bikrd,bjkd->bkrij", queries, key_rows, preferred_element_type=jnp.float32)
            * inv_root
        )
        scores = jnp.where(causal, scores, MASKED)
        return jax.nn.log_softmax(scores, axis=-1)

    query_student, key_student = split_heads(qk_student)
    query_teacher, key_teacher = split_heads(qk_teacher)
    spread = jnp.exp(log_probs(query_student, key_student)) - jnp.exp(
        log_probs(query_teacher, key_teacher)
    )
    rounded = (jnp.where(causal, spread, 0.0) / HEADS).astype(jnp.bfloat16)
    query_grad = (
        jnp.einsum("bkrij,bjkd->bikrd", rounded, key_student, preferred_element_type=jnp.float32)
        * inv_root
    )
    key_grad = (
        jnp.einsum("bkrij,bikrd->bjkd", rounded, query_student, preferred_element_type=jnp.float32)
        * inv_root
    )
    return jnp.concatenate(
        [query_grad.reshape(row_count, HEADS * HD), key_grad.reshape(row_count, KVH * HD)], axis=1
    )


def project_with(rows_in, shard_rows):
    return lax.dot_general(
        rows_in, shard_rows, (((1,), (1,)), ((), ())), preferred_element_type=jnp.float32
    )


def per_device(tokens, student_weight, snapshot, moment_one, moment_two):
    own_tokens = tokens[0]
    master = student_weight[0]
    student_copy = master.astype(jnp.bfloat16)
    cosine, sine_table = rotary_tables(own_tokens.shape[0], SEQ, HD)
    teacher_piece = shifted(snapshot, "blk", 1)[0]
    raw_student = project_with(own_tokens, lax.all_gather(student_copy, "fsdp", axis=0, tiled=True))
    raw_teacher = project_with(
        own_tokens, lax.all_gather(teacher_piece, "fsdp", axis=0, tiled=True)
    )
    qk_teacher = rotate(raw_teacher, cosine, sine_table, 1.0).astype(jnp.bfloat16)
    qk_student = rotate(raw_student, cosine, sine_table, 1.0).astype(jnp.bfloat16)
    proj_grad = rotate(score_gradient(qk_student, qk_teacher), cosine, sine_table, -1.0).astype(
        jnp.bfloat16
    )
    gradient = lax.psum_scatter(
        lax.dot_general(
            proj_grad, own_tokens, (((0,), (0,)), ((), ())), preferred_element_type=jnp.float32
        ),
        "fsdp",
        scatter_dimension=0,
        tiled=True,
    )
    first_new = BETA_ONE * moment_one[0] + (1.0 - BETA_ONE) * gradient
    second_new = BETA_TWO * moment_two[0] + (1.0 - BETA_TWO) * gradient * gradient
    step_dir = (
        first_new
        / (1.0 - BETA_ONE**STEP)
        / (jnp.sqrt(second_new / (1.0 - BETA_TWO**STEP)) + EPSILON)
    )
    updated = master - LEARN_RATE * (step_dir + DECAY * master)
    return (updated[None], first_new[None], second_new[None])


def solution(mesh):
    return jax.shard_map(
        per_device,
        mesh=mesh,
        in_specs=(
            P("blk", "fsdp", None),
            P("blk", "fsdp", None),
            P("blk", "fsdp", None),
            P("blk", "fsdp", None),
            P("blk", "fsdp", None),
        ),
        out_specs=(P("blk", "fsdp", None), P("blk", "fsdp", None), P("blk", "fsdp", None)),
        check_vma=False,
    )
```

profile of v0, /device:TPU:19, one launch (start us, length us, event | category | flops | bytes accessed | tf_op | source)
XLA Modules:
  0.0 554.5 jit_solution(4404483493618651479)
XLA Ops:
  7.2 3.1 bitcast_convert_fusion
  10.4 1.3 collective-permute-start
  11.7 28.6 %collective-permute-done = bf16[1,320,2048]{2,1,0:T(8,128)(2,1)S(1)} collective-permute-done((bf16[1,320,2048]{2,1,0:T(8,128)(2,1)}, bf16[1,320,2048]{2,1,0:T(8,128)(2,1)S(1)}, u32[]{:S(2)}, u32[]{:S(2)}) %collective-permute-start) | collective-permute-done | bytes 1310752 | tf_op jit(solution)/shard_map/ppermute | solution.py:27
  42.1 67.7 %all-gather.4.cloned.1.call-done = bf16[2560,2048]{1,0:T(8,128)(2,1)} async-done(((bf16[320,2048]{1,0:T(8,128)(2,1)}), bf16[2560,2048]{1,0:T(8,128)(2,1)}) %all-gather.4.cloned.1.call-update) | async-done | bytes 10485776 | tf_op jit(solution)/shard_map/all_gather | solution.py:105
  109.8 9.8 %fusion.32 = f32[512,20,128]{0,2,1:T(8,128)} fusion(bf16[20,128,2048]{2,1,0:T(8,128)(2,1)} %bitcast.116, bf16[1,512,2048]{2,1,0:T(8,128)(2,1)S(1)} %copy-done), kind=kOutput, calls=%fused_computation.52 | convolution fusion | flops 5368709120 | bytes 17825792 | tf_op jit(solution)/shard_map/dot_general | solution.py:94
  119.6 90.2 %all-gather.6.cloned.1.call-done = bf16[1,2560,2048]{2,1,0:T(8,128)(2,1)} async-done(((bf16[1,320,2048]{2,1,0:T(8,128)(2,1)}), bf16[1,2560,2048]{2,1,0:T(8,128)(2,1)}) %all-gather.6.cloned.1.call-update) | async-done | bytes 10485776 | tf_op jit(solution)/shard_map/all_gather | solution.py:107
  209.8 8.6 %fusion.30 = f32[512,20,128]{0,2,1:T(8,128)S(1)} fusion(bf16[20,128,2048]{2,1,0:T(8,128)(2,1)} %bitcast.117, bf16[1,512,2048]{2,1,0:T(8,128)(2,1)S(1)} %copy-done), kind=kOutput, calls=%fused_computation.50 | convolution fusion | flops 5368709120 | bytes 17825792 | tf_op jit(solution)/shard_map/dot_general | solution.py:94
  218.5 2.0 subtract_convert_fusion.2
  221.1 1.5 slice.47
  222.6 1.5 slice.43
  224.1 4.0 reshape.133
  228.9 1.7 copy.46
  230.6 6.1 %fusion.28 = f32[2,4,256,256,4]{3,2,4,1,0:T(8,128)} fusion(bf16[2,256,4,4,128]{1,0,4,3,2:T(2,128)(2,1)} %reshape.133, bf16[2,256,4,128,1]{3,2,1,0,4:T(4,128)(2,1)S(1)} %bitcast.115), kind=kOutput, calls=%fused_computation.48 | convolution fusion | flops 536870912 | bytes 11010048 | tf_op jit(solution)/shard_map/bikrd,bjkd->bkrij/dot_general | solution.py:68
  236.7 12.7 %fusion = f32[2,4,4,256,256]{3,4,2,1,0:T(8,128)} fusion(f32[2,4,256,256,4]{3,2,4,1,0:T(8,128)} %fusion.28, pred[256,256]{0,1:T(8,128)(4,1)S(1)} %iota_compare_fusion), kind=kOutput, calls=%fused_computation | output fusion | flops 10502654 | bytes 16842752 | tf_op jit(solution)/shard_map/jit(log_softmax)/reduce_sum | solution.py:72
  249.4 11.6 %fusion.15 = f32[2,4,4,256,256]{3,4,2,1,0:T(8,128)} fusion(f32[2,4,256,256,4]{3,2,4,1,0:T(8,128)} %fusion.28, pred[256,256]{0,1:T(8,128)(4,1)S(1)} %iota_compare_fusion), kind=kOutput, calls=%fused_computation.21 | output fusion | flops 10494207 | bytes 16842752 | tf_op jit(solution)/shard_map/jit(log_softmax)/sub | solution.py:72
  261.0 4.0 reshape.131
  265.1 1.5 copy.43
  267.9 2.9 fusion.36
  270.7 4.9 fusion.13
  275.7 13.6 %fusion.8 = bf16[2,4,4,256,256]{3,4,2,1,0:T(8,128)(2,1)S(1)} fusion(f32[2,4,4,256,256]{3,4,2,1,0:T(8,128)} %fusion.15, f32[2,4,4,256,256]{3,4,2,1,0:T(8,128)} %fusion, f32[2,4,4,256,256]{3,4,2,1,0:T(8,128)} %fusion.13, pred[256,256]{0,1:T(8,128)(4,1)S(1)} %iota_compare_fusion), kind=kOutput, calls=%fused_computation.9 | output fusion | flops 12591359 | bytes 29425664 | tf_op jit(solution)/shard_map/jit(log_softmax)/reduce_sum | solution.py:72
  289.3 2.5 fusion.46
  291.8 2.8 multiply_bitcast_fusion
  294.5 5.4 copy.22
  300.0 5.6 %reshape.120 = f32[512,2048]{1,0:T(8,128)} reshape(f32[2,256,4,4,128]{4,3,2,1,0:T(4,128)} %copy.22) | data formatting | bytes 8388608 | tf_op jit(solution)/shard_map/reshape | solution.py:89
  305.6 1.3 copy.25
  306.9 1.3 copy.66
  308.2 4.9 pad_maximum_fusion
  313.1 5.9 %copy.26 = f32[512,2560]{0,1:T(8,128)} copy(f32[512,2560]{1,0:T(8,128)} %pad_maximum_fusion) | data formatting | bytes 10485760 | tf_op jit(solution)/shard_map/concatenate | solution.py:88
  319.1 3.4 subtract_convert_fusion
  322.7 10.0 %fusion.34 = f32[2560,2048]{1,0:T(8,128)} fusion(bf16[512,2560]{0,1:T(8,128)(2,1)S(1)} %bitcast.113, bf16[1,512,2048]{2,1,0:T(8,128)(2,1)S(1)} %copy-done), kind=kOutput, calls=%fused_computation.54 | convolution fusion | flops 5368709120 | bytes 25690112 | tf_op jit(solution)/shard_map/dot_general | solution.py:115
  332.7 205.8 %reduce-scatter.2.cloned.1.call-done = f32[320,2048]{1,0:T(8,128)} async-done(((f32[2560,2048]{1,0:T(8,128)}), f32[320,2048]{1,0:T(8,128)}) %reduce-scatter.2.cloned.1.call-update) | async-done | bytes 2621456 | tf_op jit(solution)/shard_map/reduce_scatter | solution.py:114
  538.5 9.5 %fusion.50 = (f32[1,320,2048]{2,1,0:T(8,128)}, f32[1,320,2048]{2,1,0:T(8,128)}, f32[1,320,2048]{2,1,0:T(8,128)}) fusion(f32[320,2048]{1,0:T(8,128)} %reduce-scatter.2.cloned.1.call-done, f32[1,320,2048]{2,1,0:T(8,128)} %param.10, f32[1,320,2048]{2,1,0:T(8,128)} %param.9, f32[1,320,2048]{2,1,0:T(8,128)} %param.7), kind=kLoop, calls=%fused_computation.65 | loop fusion | flops 9830400 | bytes 18350080 | tf_op jit(solution)/shard_map/broadcast_in_dim | solution.py:130
  (30 shorter events, 5.1 us)
Async XLA Ops:
  7.2 102.6 %copy-start = (bf16[1,512,2048]{2,1,0:T(8,128)(2,1)S(1)}, bf16[1,512,2048]{2,1,0:T(8,128)(2,1)}, u32[]{:S(2)}) copy-start(bf16[1,512,2048]{2,1,0:T(8,128)(2,1)} %param.6) | copy-start | bytes 6291460
  7.2 102.6 %all-gather.4.cloned.1.call-start = ((), (), s32[]{:S(2)}) async-start(), calls=%async_computation.1 | async-start | bytes 11796480 | tf_op jit(solution)/shard_map/all_gather | solution.py:105
  10.4 199.4 %all-gather.6.cloned.1.call-start = ((), (), s32[]{:S(2)}) async-start(), calls=%async_computation.3 | async-start | bytes 11796480 | tf_op jit(solution)/shard_map/all_gather | solution.py:107
  10.4 29.9 %collective-permute-start = (bf16[1,320,2048]{2,1,0:T(8,128)(2,1)}, bf16[1,320,2048]{2,1,0:T(8,128)(2,1)S(1)}, u32[]{:S(2)}, u32[]{:S(2)}) collective-permute-start(bf16[1,320,2048]{2,1,0:T(8,128)(2,1)} %param.8), channel_id=1, source_target_pairs={{0,8},{8,16},{16,24},{24,0},{1,9},{9,17},{17,25},{25,1},{2,10},{10... | collective-permute-start | bytes 3932168 | tf_op jit(solution)/shard_map/ppermute | solution.py:27
  40.3 1.1 copy-start.3
  41.4 497.1 %reduce-scatter.2.cloned.1.call-start = ((), (), s32[]{:S(2)}) async-start(), calls=%async_computation.2 | async-start | bytes 23592960 | tf_op jit(solution)/shard_map/reduce_scatter | solution.py:114
  209.8 8.6 %slice-start = ((s8[5242880]{0:T(1024)(128)(4,1)}), s8[4194304]{0:T(1024)(128)(4,1)S(1)}, s32[]{:S(2)}) async-start(s8[5242880]{0:T(1024)(128)(4,1)} %bitcast.109), calls=%async_computation.4 | async-start | bytes 8388608
  209.8 8.6 %slice-start.1 = ((s8[5242880]{0:T(1024)(128)(4,1)}), s8[1048576]{0:T(1024)(128)(4,1)S(1)}, s32[]{:S(2)}) async-start(s8[5242880]{0:T(1024)(128)(4,1)} %bitcast.109), calls=%async_computation.5 | async-start | bytes 2097152
  275.7 13.6 %copy-start.1 = (bf16[2,256,4,4,128]{1,0,4,3,2:T(2,128)(2,1)S(1)}, bf16[2,256,4,4,128]{1,0,4,3,2:T(2,128)(2,1)}, u32[]{:S(2)}) copy-start(bf16[2,256,4,4,128]{1,0,4,3,2:T(2,128)(2,1)} %reshape.131) | copy-start | bytes 6291460
  300.0 5.6 %copy-start.2 = (f32[2,256,4,128]{1,3,2,0:T(8,128)S(1)}, f32[2,256,4,128]{1,3,2,0:T(8,128)}, u32[]{:S(2)}) copy-start(f32[2,256,4,128]{1,3,2,0:T(8,128)} %fusion.46) | copy-start | bytes 3145732
Sparse Core Ops, SparseCore 0:
  10.5 99.2 all-gather.3
  112.0 97.7 all-gather.5
  332.8 205.6 reduce-scatter.1
where the time goes:
time: 559 us; the launch traced here: 555 us
  waiting for transfers between devices  392 us (70%)
  other arithmetic  67.2 us (12%)
  matrix products  42.6 us (8%)
  local copies, waits for them, and re-layouts  37 us (7%)
  between operations  13.9 us (2%)
    reduce_scatter x1, waiting for transfers between devices, per_device(): lax.psum_scatter(lax.dot_general(proj_grad, own_tokens, (((0,), (0,)), ((...  206 us
    all_gather x1, waiting for transfers between devices, per_device(): lax.all_gather(teacher_piece, 'fsdp', axis=0, tiled=True)  90.2 us
    all_gather x1, waiting for transfers between devices, per_device(): lax.all_gather(student_copy, 'fsdp', axis=0, tiled=True)  67.7 us
    ppermute x1, waiting for transfers between devices, shifted(): return lax.ppermute(value, axis, pairs)  28.6 us
    reduce_sum x2, other arithmetic, log_probs(): return jax.nn.log_softmax(scores, axis=-1)  26.3 us
    dot_general x2, matrix products, project_with(): lax.dot_general(rows_in, shard_rows, (((1,), (1,)), ((), ())), preferred_...  18.4 us
    sub x2, other arithmetic, log_probs(): return jax.nn.log_softmax(scores, axis=-1)  16.5 us
  transfers between devices with their start and end apart: 4, of which 4 were waited for; matrix products, arithmetic and copies ran while one was open for 2% of the time, Pallas kernels for 0%

commit v1 on v0

v1 whole, which is shorter than its diff:
```python
import functools
import math

import jax
import jax.numpy as jnp
from jax import lax
from jax.experimental import pallas as pl
from jax.experimental.pallas import tpu as pltpu
from jax.sharding import PartitionSpec as P

HEADS = 16
KVH = 4
HD = 128
SEQ = 256
STEP = 100
GROUP = HEADS // KVH
HEAD_ROWS = (GROUP + 1) * HD
UNITS = GROUP + 1

THETA = 500000.0
BETA_ONE = 0.9
BETA_TWO = 0.95
LEARN_RATE = 0.002
DECAY = 0.1
EPSILON = 1e-08
MASKED = -1e30
MESH = pl.DeviceIdType.MESH


def rotary_tables():
    positions = jnp.arange(SEQ).astype(jnp.float32)
    exponents = jnp.arange(HD // 2).astype(jnp.float32) * (2.0 / HD)
    angles = positions[:, None] * (THETA ** (-exponents))[None, :]
    cosine, sine = jnp.cos(angles), jnp.sin(angles)
    return (
        jnp.concatenate([cosine, cosine], axis=1),
        jnp.concatenate([-sine, sine], axis=1),
    )


def sequence_grad(x, w_student, w_teacher, cosine, sine):
    inv_root = 1.0 / math.sqrt(HD)

    def project(weight):
        raw = lax.dot_general(
            x, weight, (((1,), (1,)), ((), ())), preferred_element_type=jnp.float32
        )
        parts = []
        for head in range(GROUP + 1):
            part = raw[:, head * HD : (head + 1) * HD]
            turned = part * cosine + pltpu.roll(part, HD // 2, 1) * sine
            parts.append(turned.astype(jnp.bfloat16))
        return parts

    student, teacher = project(w_student), project(w_teacher)
    rows = lax.broadcasted_iota(jnp.int32, (SEQ, SEQ), 0)
    columns = lax.broadcasted_iota(jnp.int32, (SEQ, SEQ), 1)
    causal = rows >= columns

    def probs(query, key):
        scores = (
            lax.dot_general(
                query, key, (((1,), (1,)), ((), ())), preferred_element_type=jnp.float32
            )
            * inv_root
        )
        scores = jnp.where(causal, scores, MASKED)
        spread = jnp.exp(scores - jnp.max(scores, axis=-1, keepdims=True))
        return spread * (1.0 / jnp.sum(spread, axis=-1, keepdims=True))

    def turn_back(part):
        return (part * cosine - pltpu.roll(part, HD // 2, 1) * sine).astype(jnp.bfloat16)

    pieces = []
    key_grad = jnp.zeros((SEQ, HD), jnp.float32)
    for head in range(GROUP):
        spread = probs(student[head], student[GROUP]) - probs(teacher[head], teacher[GROUP])
        rounded = (jnp.where(causal, spread, 0.0) * (1.0 / HEADS)).astype(jnp.bfloat16)
        query_grad = jnp.dot(rounded, student[GROUP], preferred_element_type=jnp.float32)
        pieces.append(turn_back(query_grad * inv_root))
        key_grad += lax.dot_general(
            rounded, student[head], (((0,), (0,)), ((), ())), preferred_element_type=jnp.float32
        )
    pieces.append(turn_back(key_grad * inv_root))
    return jnp.concatenate(pieces, axis=1)


def kernel(
    n, blocks, seqs,
    tokens, student, teacher, cos_ref, sin_ref, out,
    held, weight, total, partial,
    w_send, w_recv, s_send, s_recv, t_send, t_recv, g_send, g_recv, f_send, f_recv,
):
    share = n // KVH
    me, blk = lax.axis_index("fsdp"), lax.axis_index("blk")
    chip, lane = lax.div(me, share), lax.rem(me, share)

    def placed(native):
        is_key = lax.div(native, HEADS * share)
        key = (native - HEADS * share) * is_key
        head = (1 - is_key) * lax.div(native, GROUP * share) + is_key * lax.div(key, share)
        at = (1 - is_key) * lax.rem(native, GROUP * share) + is_key * (
            GROUP * share + lax.rem(key, share)
        )
        return head * (UNITS * share) + at

    def native_of(place):
        head, at = lax.div(place, UNITS * share), lax.rem(place, UNITS * share)
        is_key = lax.div(at, GROUP * share)
        return (1 - is_key) * (GROUP * share * head + at) + is_key * (
            HEADS * share + share * head + at - GROUP * share
        )

    def each(count, body):
        def run(step, carry):
            body(step)
            return carry

        lax.fori_loop(0, count, run, 0)

    def landed(ref, sem):
        pltpu.make_async_copy(ref, ref, sem).wait()

    def to(src, dst, send_sem, recv_sem, device, group=None):
        target = {"fsdp": device, "blk": blk if group is None else group}
        return pltpu.make_async_remote_copy(
            src_ref=src, dst_ref=dst, send_sem=send_sem, recv_sem=recv_sem,
            device_id=target, device_id_type=MESH,
        )

    for seq in range(seqs):
        pltpu.make_async_copy(tokens.at[seq], held.at[chip, seq], t_recv.at[chip, seq]).start()

    barrier = pltpu.get_barrier_semaphore()
    after = lax.rem(blk + 1, blocks)
    before = lax.rem(blk + blocks - 1, blocks)

    def greet(step):
        pl.semaphore_signal(
            barrier, inc=1, device_id={"fsdp": lax.rem(me + 1 + step, n), "blk": blk},
            device_id_type=MESH,
        )

    def greet_teacher(unit):
        source = lax.div(native_of(me * UNITS + unit), UNITS)
        pl.semaphore_signal(
            barrier, inc=1, device_id={"fsdp": source, "blk": before}, device_id_type=MESH
        )

    each(n - 1, greet)
    each(UNITS, greet_teacher)
    pl.semaphore_wait(barrier, n - 1 + UNITS)

    def send_rows(unit):
        place = placed(me * UNITS + unit)
        device, slot = lax.div(place, UNITS), lax.rem(place, UNITS)
        at = lax.rem(place, UNITS * share)

        @pl.when(device == me)
        def _():
            pltpu.make_async_copy(
                student.at[unit], weight.at[0, at], w_recv.at[0, slot]
            ).start()

        @pl.when(device != me)
        def _():
            to(
                student.at[unit], weight.at[0, at], w_send.at[0, unit], w_recv.at[0, slot], device
            ).start()

        to(
            teacher.at[unit], weight.at[1, at], w_send.at[1, unit], w_recv.at[1, slot], device,
            after,
        ).start()

    each(UNITS, send_rows)

    def pass_right(src, slot, seq):
        return to(src, held.at[slot, seq], t_send.at[0, slot, seq], t_recv.at[slot, seq], me + share)

    def pass_left(src, slot, seq):
        return to(src, held.at[slot, seq], t_send.at[1, slot, seq], t_recv.at[slot, seq], me - share)

    for seq in range(seqs):

        @pl.when(chip < KVH - 1)
        def _():
            pass_right(tokens.at[seq], chip, seq).start()

        @pl.when(chip > 0)
        def _():
            pass_left(tokens.at[seq], chip, seq).start()

    total[...] = jnp.zeros_like(total)

    def sibling(step):
        return chip * share + lax.rem(lane + step, share)

    for which in range(2):
        each(
            UNITS,
            lambda unit: landed(weight.at[which, lane * UNITS + unit], w_recv.at[which, unit]),
        )
        mine = weight.at[which, pl.ds(lane * UNITS, UNITS)]
        for step in range(1, share):
            to(
                mine, mine, s_send.at[which, step - 1], s_recv.at[which, step - 1], sibling(step)
            ).start()
    for which in range(2):
        for step in range(1, share):
            lane_from = lax.rem(lane + share - step, share)
            landed(
                weight.at[which, pl.ds(lane_from * UNITS, UNITS)], s_recv.at[which, step - 1]
            )

    def work(step):
        seq = lax.rem(step, seqs)
        distance = lax.div(step, 2 * seqs)
        side = lax.rem(lax.div(step, seqs), 2)
        slot = chip - distance + 2 * distance * side
        valid = (distance + 1 - side > 0) & (slot >= 0) & (slot < KVH)

        @pl.when(valid)
        def _():
            landed(held.at[slot, seq], t_recv.at[slot, seq])

            @pl.when((distance > 0) & (side == 0) & (chip < KVH - 1))
            def _():
                pass_right(held.at[slot, seq], slot, seq).start()

            @pl.when((distance > 0) & (side == 1) & (chip > 0))
            def _():
                pass_left(held.at[slot, seq], slot, seq).start()

            x = held[slot, seq]
            grad = sequence_grad(
                x,
                weight[0].reshape(HEAD_ROWS, -1),
                weight[1].reshape(HEAD_ROWS, -1),
                cos_ref[...],
                sin_ref[...],
            )
            width = 512
            for start in range(0, x.shape[1], width):
                piece = lax.dot_general(
                    grad, x[:, start : start + width], (((0,), (0,)), ((), ())),
                    preferred_element_type=jnp.float32,
                )
                total[:, :, start : start + width] += piece.reshape(UNITS * share, -1, width)

    each(2 * KVH * seqs, work)

    def send_partial(unit):
        for step in range(1, share):
            lane_to = lax.rem(lane + step, share)
            to(
                total.at[lane_to * UNITS + unit], partial.at[step - 1, unit],
                g_send.at[step - 1, unit], g_recv.at[step - 1, unit], sibling(step),
            ).start()

    each(UNITS, send_partial)

    def send_sum(unit):
        at = lane * UNITS + unit
        native = native_of(me * UNITS + unit)
        device, slot = lax.div(native, UNITS), lax.rem(native, UNITS)
        for step in range(1, share):
            landed(partial.at[step - 1, unit], g_recv.at[step - 1, unit])
            total[at] += partial[step - 1, unit]

        @pl.when(device == me)
        def _():
            pltpu.make_async_copy(total.at[at], out.at[slot], f_recv.at[slot]).start()

        @pl.when(device != me)
        def _():
            to(total.at[at], out.at[slot], f_send.at[unit], f_recv.at[slot], device).start()

    each(UNITS, send_sum)

    each(UNITS, lambda unit: landed(out.at[unit], f_recv.at[unit]))

    def sent(unit):
        place = placed(me * UNITS + unit)

        @pl.when(lax.div(place, UNITS) != me)
        def _():
            landed(student.at[unit], w_send.at[0, unit])

        landed(teacher.at[unit], w_send.at[1, unit])
        for step in range(1, share):
            landed(partial.at[step - 1, unit], g_send.at[step - 1, unit])

        @pl.when(lax.div(native_of(me * UNITS + unit), UNITS) != me)
        def _():
            landed(out.at[unit], f_send.at[unit])

    each(UNITS, sent)
    for which in range(2):
        for step in range(1, share):
            landed(weight.at[which, pl.ds(lane * UNITS, UNITS)], s_send.at[which, step - 1])

    def sent_tokens(step):
        slot, seq = lax.div(step, seqs), lax.rem(step, seqs)

        @pl.when((slot <= chip) & (chip < KVH - 1))
        def _():
            landed(held.at[slot, seq], t_send.at[0, slot, seq])

        @pl.when((slot >= chip) & (chip > 0))
        def _():
            landed(held.at[slot, seq], t_send.at[1, slot, seq])

    each(KVH * seqs, sent_tokens)


def gradient_rows(tokens, student_copy, snapshot, n, blocks):
    rows, width = student_copy.shape
    seqs = tokens.shape[0] // SEQ
    share = n // KVH
    unit = rows // UNITS
    cosine, sine = rotary_tables()
    dma = pltpu.SemaphoreType.DMA
    anywhere, vmem = pl.BlockSpec(memory_space=pl.ANY), pl.BlockSpec(memory_space=pltpu.VMEM)
    gradient = pl.pallas_call(
        functools.partial(kernel, n, blocks, seqs),
        out_shape=jax.ShapeDtypeStruct((UNITS, unit, width), jnp.float32),
        in_specs=[anywhere, anywhere, anywhere, vmem, vmem],
        out_specs=vmem,
        scratch_shapes=[
            pltpu.VMEM((KVH, seqs, SEQ, width), jnp.bfloat16),
            pltpu.VMEM((2, UNITS * share, unit, width), jnp.bfloat16),
            pltpu.VMEM((UNITS * share, unit, width), jnp.float32),
            pltpu.VMEM((share - 1, UNITS, unit, width), jnp.float32),
            dma((2, UNITS)),
            dma((2, UNITS)),
            dma((2, share - 1)),
            dma((2, share - 1)),
            dma((2, KVH, seqs)),
            dma((KVH, seqs)),
            dma((share - 1, UNITS)),
            dma((share - 1, UNITS)),
            dma((UNITS,)),
            dma((UNITS,)),
        ],
        compiler_params=pltpu.CompilerParams(
            collective_id=0, has_side_effects=True, vmem_limit_bytes=56 * 1024 * 1024
        ),
    )(
        tokens.reshape(seqs, SEQ, width),
        student_copy.reshape(UNITS, unit, width),
        snapshot.reshape(UNITS, unit, width),
        cosine,
        sine,
    )
    return gradient.reshape(rows, width)


def per_device(n, blocks, tokens, student_weight, snapshot, moment_one, moment_two):
    master = student_weight[0]
    gradient = gradient_rows(tokens[0], master.astype(jnp.bfloat16), snapshot[0], n, blocks)
    first_new = BETA_ONE * moment_one[0] + (1.0 - BETA_ONE) * gradient
    second_new = BETA_TWO * moment_two[0] + (1.0 - BETA_TWO) * gradient * gradient
    step_dir = (
        first_new
        / (1.0 - BETA_ONE**STEP)
        / (jnp.sqrt(second_new / (1.0 - BETA_TWO**STEP)) + EPSILON)
    )
    updated = master - LEARN_RATE * (step_dir + DECAY * master)
    return (updated[None], first_new[None], second_new[None])


def solution(mesh):
    spec = P("blk", "fsdp", None)
    return jax.shard_map(
        functools.partial(per_device, mesh.shape["fsdp"], mesh.shape["blk"]),
        mesh=mesh,
        in_specs=(spec,) * 5,
        out_specs=(spec,) * 3,
        check_vma=False,
    )
```

time: 559 us -> 252 us (0.45)
  waiting for transfers between devices: 392 us -> 0 us
  Pallas kernels: 0 us -> 240 us
  other arithmetic: 67.2 us -> 11.2 us
  matrix products: 42.6 us -> 0 us
  local copies, waits for them, and re-layouts: 37 us -> 0.01 us
  between operations: 13.9 us -> 0.68 us
    pallas_call x0 -> x1, Pallas kernels: none -> 240 us  [gradient_rows(): pl.pallas_call(functools.partial(kernel, n, blocks, seqs), out_shape=jax....]
    reduce_scatter x1 -> x0, waiting for transfers between devices: 206 us -> none  [per_device(): lax.psum_scatter(lax.dot_general(proj_grad, own_tokens, (((0,), (0,)), ((...]
    all_gather x2 -> x0, waiting for transfers between devices: 158 us -> none  [the longest x1 90.2 us: per_device(): lax.all_gather(teacher_piece, 'fsdp', axis=0, tiled=True)]
    dot_general x7 -> x0, matrix products: 42.6 us -> none  [the longest x2 18.4 us: project_with(): lax.dot_general(rows_in, shard_rows, (((1,), (1,)), ((), ())), preferred_...]
    ppermute x1 -> x0, waiting for transfers between devices: 28.6 us -> none  [shifted(): return lax.ppermute(value, axis, pairs)]
    reduce_sum x2 -> x0, other arithmetic: 26.3 us -> none  [log_probs(): return jax.nn.log_softmax(scores, axis=-1)]
    reshape x8 -> x0, local copies, waits for them, and re-layouts: 19 us -> none  [the longest x2 7.91 us: split_heads(): packed[:, :HEADS * HD].reshape(seq_count, SEQ, KVH, group_size, HD)]
    sub x2 -> x1, other arithmetic: 16.5 us -> 6.68 us  [per_device(): updated = master - LEARN_RATE * (step_dir + DECAY * master)]
  transfers between devices with their start and end apart: 4 -> 0, of which waited for: 4 -> 0; matrix products, arithmetic and copies ran while one was open for 2% -> 0% of each run, Pallas kernels for 0% -> 0%
where the time goes in v1:
time: 252 us
  Pallas kernels  240 us (95%)
  other arithmetic  11.2 us (4%)
    pallas_call x1, Pallas kernels, gradient_rows(): pl.pallas_call(functools.partial(kernel, n, blocks, seqs), out_shape=jax....  240 us
    sub x1, other arithmetic, per_device(): updated = master - LEARN_RATE * (step_dir + DECAY * master)  6.68 us

profile of v1, /device:TPU:19, one launch (start us, length us, event | category | flops | bytes accessed | tf_op | source)
XLA Modules:
  0.0 251.7 jit_solution(5911369636420986480)
XLA Ops:
  0.7 0.5 fusion.2
  1.2 0.8 pad_maximum_fusion
  2.0 0.0 copy-start.2
  2.0 3.1 %convert_element_type.33 = bf16[1,320,2048]{2,1,0:T(8,128)(2,1)} convert(f32[1,320,2048]{2,1,0:T(8,128)} %param.6) | non-fusion elementwise | flops 655360 | bytes 3932160 | tf_op jit(solution)/shard_map/convert_element_type | solution.py:361
  5.2 0.0 copy-start
  5.2 0.0 copy-start.1
  5.2 239.9 %shard_map.76 = f32[5,64,2048]{2,1,0:T(8,128)} custom-call(bf16[2,256,2048]{2,1,0:T(8,128)(2,1)} %bitcast.12, bf16[5,64,2048]{2,1,0:T(8,128)(2,1)} %bitcast.11, bf16[5,64,2048]{2,1,0:T(8,128)(2,1)} %bitcast.13, f32[256,128]{1,0:T(8,128)} %get-tuple-element.9.cos_ref, f32[256,128]{1,0:T(8,128)} %get-tuple-element.10.sin_ref), custom_call_target="tpu_custom_call" | custom-call | tf_op jit(solution)/shard_map/pallas_call | solution.py:325
  245.0 0.0 copy-done.2
  245.1 0.0 copy-done
  245.1 0.0 copy-done.1
  245.1 6.7 %multiply_subtract_fusion = (f32[1,320,2048]{2,1,0:T(8,128)}, f32[1,320,2048]{2,1,0:T(8,128)}, f32[1,320,2048]{2,1,0:T(8,128)}) fusion(f32[1,320,2048]{2,1,0:T(8,128)S(1)} %copy-done, f32[1,320,2048]{2,1,0:T(8,128)S(1)} %copy-done.1, f32[1,320,2048]{2,1,0:T(8,128)S(1)} %copy-done.2, f32[1,320,2048]{2,1,0:T(8,128)} %bitcast.10), kind=kLoop, calls=%fused_computation.4 | loop fusion | flops 9830400 | bytes 18350080 | tf_op jit(solution)/shard_map/sub | solution.py:369
  (2 shorter events, 0.0 us)
Async XLA Ops:
  2.0 243.0 %copy-start.2 = (f32[1,320,2048]{2,1,0:T(8,128)S(1)}, f32[1,320,2048]{2,1,0:T(8,128)}, u32[]{:S(2)}) copy-start(f32[1,320,2048]{2,1,0:T(8,128)} %param.9) | copy-start | bytes 7864324
  5.2 239.9 %copy-start = (f32[1,320,2048]{2,1,0:T(8,128)S(1)}, f32[1,320,2048]{2,1,0:T(8,128)}, u32[]{:S(2)}) copy-start(f32[1,320,2048]{2,1,0:T(8,128)} %param.6) | copy-start | bytes 7864324
  5.2 239.9 %copy-start.1 = (f32[1,320,2048]{2,1,0:T(8,128)S(1)}, f32[1,320,2048]{2,1,0:T(8,128)}, u32[]{:S(2)}) copy-start(f32[1,320,2048]{2,1,0:T(8,128)} %param.8) | copy-start | bytes 7864324

commit v2 on v1

--- a/solution.py
+++ b/solution.py
@@ -88,12 +88,13 @@
 def kernel(
     n, blocks, seqs,
     tokens, student, teacher, cos_ref, sin_ref, out,
-    held, weight, total, partial,
+    held, weight, total, partial, extra,
     w_send, w_recv, s_send, s_recv, t_send, t_recv, g_send, g_recv, f_send, f_recv,
 ):
     share = n // KVH
     me, blk = lax.axis_index("fsdp"), lax.axis_index("blk")
     chip, lane = lax.div(me, share), lax.rem(me, share)
+    last, helper, split = KVH - 1, KVH - 2, KVH - 2
 
     def placed(native):
         is_key = lax.div(native, HEADS * share)
@@ -141,37 +142,44 @@
             device_id_type=MESH,
         )
 
-    def greet_teacher(unit):
-        source = lax.div(native_of(me * UNITS + unit), UNITS)
+    def greet_teacher(step):
         pl.semaphore_signal(
-            barrier, inc=1, device_id={"fsdp": source, "blk": before}, device_id_type=MESH
+            barrier, inc=1, device_id={"fsdp": step, "blk": before}, device_id_type=MESH
         )
 
     each(n - 1, greet)
-    each(UNITS, greet_teacher)
-    pl.semaphore_wait(barrier, n - 1 + UNITS)
+    each(n, greet_teacher)
+    pl.semaphore_wait(barrier, 2 * n - 1)
 
     def send_rows(unit):
         place = placed(me * UNITS + unit)
-        device, slot = lax.div(place, UNITS), lax.rem(place, UNITS)
+        owner, slot = lax.div(place, UNITS), lax.rem(place, UNITS)
         at = lax.rem(place, UNITS * share)
 
-        @pl.when(device == me)
-        def _():
-            pltpu.make_async_copy(
-                student.at[unit], weight.at[0, at], w_recv.at[0, slot]
+        def send(role, device):
+            @pl.when(device == me)
+            def _():
+                pltpu.make_async_copy(
+                    student.at[unit], weight.at[role, 0, at], w_recv.at[role, 0, slot]
+                ).start()
+
+            @pl.when(device != me)
+            def _():
+                to(
+                    student.at[unit], weight.at[role, 0, at], w_send.at[role, 0, unit],
+                    w_recv.at[role, 0, slot], device,
+                ).start()
+
+            to(
+                teacher.at[unit], weight.at[role, 1, at], w_send.at[role, 1, unit],
+                w_recv.at[role, 1, slot], device, after,
             ).start()
 
-        @pl.when(device != me)
-        def _():
-            to(
-                student.at[unit], weight.at[0, at], w_send.at[0, unit], w_recv.at[0, slot], device
-            ).start()
-
-        to(
-            teacher.at[unit], weight.at[1, at], w_send.at[1, unit], w_recv.at[1, slot], device,
-            after,
-        ).start()
+        send(0, owner)
+
+        @pl.when(owner >= last * share)
+        def _():
+            send(1, owner - share)
 
     each(UNITS, send_rows)
 
@@ -196,22 +204,37 @@
     def sibling(step):
         return chip * share + lax.rem(lane + step, share)
 
-    for which in range(2):
-        each(
-            UNITS,
-            lambda unit: landed(weight.at[which, lane * UNITS + unit], w_recv.at[which, unit]),
-        )
-        mine = weight.at[which, pl.ds(lane * UNITS, UNITS)]
+    def share_rows(role, which):
+        def arrived(unit):
+            landed(weight.at[role, which, lane * UNITS + unit], w_recv.at[role, which, unit])
+
+        each(UNITS, arrived)
+        mine = weight.at[role, which, pl.ds(lane * UNITS, UNITS)]
         for step in range(1, share):
             to(
-                mine, mine, s_send.at[which, step - 1], s_recv.at[which, step - 1], sibling(step)
+                mine, mine, s_send.at[role, which, step - 1], s_recv.at[role, which, step - 1],
+                sibling(step),
             ).start()
-    for which in range(2):
+
+    def shared_rows(role, which):
         for step in range(1, share):
             lane_from = lax.rem(lane + share - step, share)
             landed(
-                weight.at[which, pl.ds(lane_from * UNITS, UNITS)], s_recv.at[which, step - 1]
+                weight.at[role, which, pl.ds(lane_from * UNITS, UNITS)],
+                s_recv.at[role, which, step - 1],
             )
+
+    def each_role(body):
+        body(0)
+
+        @pl.when(chip == helper)
+        def _():
+            body(1)
+
+    for which in range(2):
+        each_role(functools.partial(share_rows, which=which))
+    for which in range(2):
+        each_role(functools.partial(shared_rows, which=which))
 
     def work(step):
         seq = lax.rem(step, seqs)
@@ -220,11 +243,11 @@
         slot = chip - distance + 2 * distance * side
         valid = (distance + 1 - side > 0) & (slot >= 0) & (slot < KVH)
 
-        @pl.when(valid)
+        @pl.when(valid & ((chip < last) | (slot >= split)))
         def _():
             landed(held.at[slot, seq], t_recv.at[slot, seq])
 
-            @pl.when((distance > 0) & (side == 0) & (chip < KVH - 1))
+            @pl.when((distance > 0) & (side == 0) & (chip < helper))
             def _():
                 pass_right(held.at[slot, seq], slot, seq).start()
 
@@ -232,78 +255,123 @@
             def _():
                 pass_left(held.at[slot, seq], slot, seq).start()
 
-            x = held[slot, seq]
-            grad = sequence_grad(
-                x,
-                weight[0].reshape(HEAD_ROWS, -1),
-                weight[1].reshape(HEAD_ROWS, -1),
-                cos_ref[...],
-                sin_ref[...],
-            )
-            width = 512
-            for start in range(0, x.shape[1], width):
-                piece = lax.dot_general(
-                    grad, x[:, start : start + width], (((0,), (0,)), ((), ())),
-                    preferred_element_type=jnp.float32,
+            def add_gradient(role):
+                x = held[slot, seq]
+                grad = sequence_grad(
+                    x,
+                    weight[role, 0].reshape(HEAD_ROWS, -1),
+                    weight[role, 1].reshape(HEAD_ROWS, -1),
+                    cos_ref[...],
+                    sin_ref[...],
                 )
-                total[:, :, start : start + width] += piece.reshape(UNITS * share, -1, width)
+                width = 512
+                for start in range(0, x.shape[1], width):
+                    piece = lax.dot_general(
+                        grad, x[:, start : start + width], (((0,), (0,)), ((), ())),
+                        preferred_element_type=jnp.float32,
+                    )
+                    total[role, :, :, start : start + width] += piece.reshape(
+                        UNITS * share, -1, width
+                    )
+
+            roles = 1 + lax.div(chip, helper) * lax.div(KVH - 1 - slot, split) * (last - chip)
+            each(roles, add_gradient)
 
     each(2 * KVH * seqs, work)
 
-    def send_partial(unit):
-        for step in range(1, share):
-            lane_to = lax.rem(lane + step, share)
-            to(
-                total.at[lane_to * UNITS + unit], partial.at[step - 1, unit],
-                g_send.at[step - 1, unit], g_recv.at[step - 1, unit], sibling(step),
-            ).start()
-
-    each(UNITS, send_partial)
-
-    def send_sum(unit):
-        at = lane * UNITS + unit
-        native = native_of(me * UNITS + unit)
-        device, slot = lax.div(native, UNITS), lax.rem(native, UNITS)
-        for step in range(1, share):
-            landed(partial.at[step - 1, unit], g_recv.at[step - 1, unit])
-            total[at] += partial[step - 1, unit]
-
-        @pl.when(device == me)
-        def _():
-            pltpu.make_async_copy(total.at[at], out.at[slot], f_recv.at[slot]).start()
-
-        @pl.when(device != me)
-        def _():
-            to(total.at[at], out.at[slot], f_send.at[unit], f_recv.at[slot], device).start()
-
-    each(UNITS, send_sum)
-
-    each(UNITS, lambda unit: landed(out.at[unit], f_recv.at[unit]))
+    def send_partials(role):
+        def send_partial(unit):
+            for step in range(1, share):
+                lane_to = lax.rem(lane + step, share)
+                to(
+                    total.at[role, lane_to * UNITS + unit], partial.at[role, step - 1, unit],
+                    g_send.at[role, step - 1, unit], g_recv.at[role, step - 1, unit],
+                    sibling(step),
+                ).start()
+
+        each(UNITS, send_partial)
+
+    def send_sums(role):
+        landing = (out, extra)[role]
+
+        def send_sum(unit):
+            at = lane * UNITS + unit
+            native = native_of((me + role * share) * UNITS + unit)
+            device, slot = lax.div(native, UNITS), lax.rem(native, UNITS)
+            for step in range(1, share):
+                landed(partial.at[role, step - 1, unit], g_recv.at[role, step - 1, unit])
+                total[role, at] += partial[role, step - 1, unit]
+
+            @pl.when(device == me)
+            def _():
+                pltpu.make_async_copy(
+                    total.at[role, at], landing.at[slot], f_recv.at[role, slot]
+                ).start()
+
+            @pl.when(device != me)
+            def _():
+                to(
+                    total.at[role, at], landing.at[slot], f_send.at[role, unit],
+                    f_recv.at[role, slot], device,
+                ).start()
+
+        each(UNITS, send_sum)
+
+    each_role(send_partials)
+    each_role(send_sums)
+
+    def arrive(unit):
+        landed(out.at[unit], f_recv.at[0, unit])
+
+        @pl.when(placed(me * UNITS + unit) >= last * share * UNITS)
+        def _():
+            landed(extra.at[unit], f_recv.at[1, unit])
+            out[unit] += extra[unit]
+
+    each(UNITS, arrive)
 
     def sent(unit):
-        place = placed(me * UNITS + unit)
-
-        @pl.when(lax.div(place, UNITS) != me)
-        def _():
-            landed(student.at[unit], w_send.at[0, unit])
-
-        landed(teacher.at[unit], w_send.at[1, unit])
-        for step in range(1, share):
-            landed(partial.at[step - 1, unit], g_send.at[step - 1, unit])
-
-        @pl.when(lax.div(native_of(me * UNITS + unit), UNITS) != me)
-        def _():
-            landed(out.at[unit], f_send.at[unit])
+        owner = lax.div(placed(me * UNITS + unit), UNITS)
+
+        def rows_left(role, device):
+            @pl.when(device != me)
+            def _():
+                landed(student.at[unit], w_send.at[role, 0, unit])
+
+            landed(teacher.at[unit], w_send.at[role, 1, unit])
+
+        rows_left(0, owner)
+
+        @pl.when(owner >= last * share)
+        def _():
+            rows_left(1, owner - share)
+
+        def sums_left(role):
+            for step in range(1, share):
+                landed(partial.at[role, step - 1, unit], g_send.at[role, step - 1, unit])
+
+            @pl.when(lax.div(native_of((me + role * share) * UNITS + unit), UNITS) != me)
+            def _():
+                landed(out.at[unit], f_send.at[role, unit])
+
+        each_role(sums_left)
 
     each(UNITS, sent)
-    for which in range(2):
-        for step in range(1, share):
-            landed(weight.at[which, pl.ds(lane * UNITS, UNITS)], s_send.at[which, step - 1])
+
+    def shares_left(role):
+        for which in range(2):
+            for step in range(1, share):
+                landed(
+                    weight.at[role, which, pl.ds(lane * UNITS, UNITS)],
+                    s_send.at[role, which, step - 1],
+                )
+
+    each_role(shares_left)
 
     def sent_tokens(step):
         slot, seq = lax.div(step, seqs), lax.rem(step, seqs)
 
-        @pl.when((slot <= chip) & (chip < KVH - 1))
+        @pl.when((slot <= chip) & ((chip < helper) | ((chip == helper) & (slot == chip))))
         def _():
             landed(held.at[slot, seq], t_send.at[0, slot, seq])
 
@@ -329,19 +397,20 @@
         out_specs=vmem,
         scratch_shapes=[
             pltpu.VMEM((KVH, seqs, SEQ, width), jnp.bfloat16),
-            pltpu.VMEM((2, UNITS * share, unit, width), jnp.bfloat16),
-            pltpu.VMEM((UNITS * share, unit, width), jnp.float32),
-            pltpu.VMEM((share - 1, UNITS, unit, width), jnp.float32),
+            pltpu.VMEM((2, 2, UNITS * share, unit, width), jnp.bfloat16),
+            pltpu.VMEM((2, UNITS * share, unit, width), jnp.float32),
+            pltpu.VMEM((2, share - 1, UNITS, unit, width), jnp.float32),
+            pltpu.VMEM((UNITS, unit, width), jnp.float32),
+            dma((2, 2, UNITS)),
+            dma((2, 2, UNITS)),
+            dma((2, 2, share - 1)),
+            dma((2, 2, share - 1)),
+            dma((2, KVH, seqs)),
+            dma((KVH, seqs)),
+            dma((2, share - 1, UNITS)),
+            dma((2, share - 1, UNITS)),
             dma((2, UNITS)),
             dma((2, UNITS)),
-            dma((2, share - 1)),
-            dma((2, share - 1)),
-            dma((2, KVH, seqs)),
-            dma((KVH, seqs)),
-            dma((share - 1, UNITS)),
-            dma((share - 1, UNITS)),
-            dma((UNITS,)),
-            dma((UNITS,)),
         ],
         compiler_params=pltpu.CompilerParams(
             collective_id=0, has_side_effects=True, vmem_limit_bytes=56 * 1024 * 1024

time: 252 us -> 216 us (0.86)
  the two profiles are of different devices: /device:TPU:19 before, /device:TPU:1 now
where the time goes in v2:
time: 216 us
  Pallas kernels  204 us (94%)
  other arithmetic  11.2 us (5%)
    pallas_call x1, Pallas kernels, gradient_rows(): pl.pallas_call(functools.partial(kernel, n, blocks, seqs), out_shape=jax....  204 us
    sub x1, other arithmetic, per_device(): updated = master - LEARN_RATE * (step_dir + DECAY * master)  6.68 us

profile of v2, /device:TPU:1, one launch (start us, length us, event | category | flops | bytes accessed | tf_op | source)
XLA Modules:
  0.0 215.6 jit_solution(2227412840059174109)
XLA Ops:
  0.7 0.5 fusion.2
  1.2 0.8 pad_maximum_fusion
  2.0 0.0 copy-start.2
  2.0 3.1 %convert_element_type.33 = bf16[1,320,2048]{2,1,0:T(8,128)(2,1)} convert(f32[1,320,2048]{2,1,0:T(8,128)} %param.6) | non-fusion elementwise | flops 655360 | bytes 3932160 | tf_op jit(solution)/shard_map/convert_element_type | solution.py:430
  5.2 0.0 copy-start
  5.2 0.0 copy-start.1
  5.2 203.7 %shard_map.76 = f32[5,64,2048]{2,1,0:T(8,128)} custom-call(bf16[2,256,2048]{2,1,0:T(8,128)(2,1)} %bitcast.12, bf16[5,64,2048]{2,1,0:T(8,128)(2,1)} %bitcast.11, bf16[5,64,2048]{2,1,0:T(8,128)(2,1)} %bitcast.13, f32[256,128]{1,0:T(8,128)} %get-tuple-element.9.cos_ref, f32[256,128]{1,0:T(8,128)} %get-tuple-element.10.sin_ref), custom_call_target="tpu_custom_call" | custom-call | tf_op jit(solution)/shard_map/pallas_call | solution.py:393
  208.9 0.0 copy-done.2
  208.9 0.0 copy-done
  209.0 0.0 copy-done.1
  209.0 6.7 %multiply_subtract_fusion = (f32[1,320,2048]{2,1,0:T(8,128)}, f32[1,320,2048]{2,1,0:T(8,128)}, f32[1,320,2048]{2,1,0:T(8,128)}) fusion(f32[1,320,2048]{2,1,0:T(8,128)S(1)} %copy-done, f32[1,320,2048]{2,1,0:T(8,128)S(1)} %copy-done.1, f32[1,320,2048]{2,1,0:T(8,128)S(1)} %copy-done.2, f32[1,320,2048]{2,1,0:T(8,128)} %bitcast.10), kind=kLoop, calls=%fused_computation.4 | loop fusion | flops 9830400 | bytes 18350080 | tf_op jit(solution)/shard_map/sub | solution.py:438
  (2 shorter events, 0.0 us)
Async XLA Ops:
  2.0 206.9 %copy-start.2 = (f32[1,320,2048]{2,1,0:T(8,128)S(1)}, f32[1,320,2048]{2,1,0:T(8,128)}, u32[]{:S(2)}) copy-start(f32[1,320,2048]{2,1,0:T(8,128)} %param.9) | copy-start | bytes 7864324
  5.2 203.8 %copy-start = (f32[1,320,2048]{2,1,0:T(8,128)S(1)}, f32[1,320,2048]{2,1,0:T(8,128)}, u32[]{:S(2)}) copy-start(f32[1,320,2048]{2,1,0:T(8,128)} %param.6) | copy-start | bytes 7864324
  5.2 203.8 %copy-start.1 = (f32[1,320,2048]{2,1,0:T(8,128)S(1)}, f32[1,320,2048]{2,1,0:T(8,128)}, u32[]{:S(2)}) copy-start(f32[1,320,2048]{2,1,0:T(8,128)} %param.8) | copy-start | bytes 7864324

commit v3 on v2

--- a/solution.py
+++ b/solution.py
@@ -151,12 +151,12 @@
     each(n, greet_teacher)
     pl.semaphore_wait(barrier, 2 * n - 1)
 
-    def send_rows(unit):
+    def send_rows(unit, role):
         place = placed(me * UNITS + unit)
         owner, slot = lax.div(place, UNITS), lax.rem(place, UNITS)
         at = lax.rem(place, UNITS * share)
 
-        def send(role, device):
+        def send(device):
             @pl.when(device == me)
             def _():
                 pltpu.make_async_copy(
@@ -175,13 +175,19 @@
                 w_recv.at[role, 1, slot], device, after,
             ).start()
 
-        send(0, owner)
-
-        @pl.when(owner >= last * share)
-        def _():
-            send(1, owner - share)
-
-    each(UNITS, send_rows)
+        if role == 0:
+            send(owner)
+        else:
+
+            @pl.when(owner >= last * share)
+            def _():
+                send(owner - share)
+
+    each(UNITS, functools.partial(send_rows, role=0))
+
+    @pl.when(chip < last)
+    def _():
+        each(UNITS, functools.partial(send_rows, role=1))
 
     def pass_right(src, slot, seq):
         return to(src, held.at[slot, seq], t_send.at[0, slot, seq], t_recv.at[slot, seq], me + share)
@@ -231,29 +237,58 @@
         def _():
             body(1)
 
+    @pl.when(chip == last)
+    def _():
+        for seq in range(seqs):
+            landed(held.at[chip, seq], t_send.at[1, chip, seq])
+        each(UNITS, functools.partial(send_rows, role=1))
+
     for which in range(2):
-        each_role(functools.partial(share_rows, which=which))
+        share_rows(0, which)
     for which in range(2):
-        each_role(functools.partial(shared_rows, which=which))
+        shared_rows(0, which)
+
+    def chunk(step):
+        turn, seq = lax.div(step, seqs), lax.rem(step, seqs)
+        distance, side = lax.div(turn + 1, 2), lax.rem(turn, 2)
+        slot = chip - distance + 2 * distance * side
+        valid = (slot >= 0) & (slot < KVH) & ((chip < last) | (slot >= split))
+        relayed = valid & (
+            ((side == 1) & (chip > 0)) | ((side == 0) & (distance > 0) & (chip < helper))
+        )
+        return slot, seq, side, valid, relayed
+
+    def relay(step):
+        slot, seq, side, _, relayed = chunk(step)
+
+        @pl.when(relayed)
+        def _():
+            landed(held.at[slot, seq], t_recv.at[slot, seq])
+
+            @pl.when(side == 0)
+            def _():
+                pass_right(held.at[slot, seq], slot, seq).start()
+
+            @pl.when(side == 1)
+            def _():
+                pass_left(held.at[slot, seq], slot, seq).start()
 
     def work(step):
-        seq = lax.rem(step, seqs)
-        distance = lax.div(step, 2 * seqs)
-        side = lax.rem(lax.div(step, seqs), 2)
-        slot = chip - distance + 2 * distance * side
-        valid = (distance + 1 - side > 0) & (slot >= 0) & (slot < KVH)
-
-        @pl.when(valid & ((chip < last) | (slot >= split)))
-        def _():
-            landed(held.at[slot, seq], t_recv.at[slot, seq])
-
-            @pl.when((distance > 0) & (side == 0) & (chip < helper))
-            def _():
-                pass_right(held.at[slot, seq], slot, seq).start()
-
-            @pl.when((distance > 0) & (side == 1) & (chip > 0))
-            def _():
-                pass_left(held.at[slot, seq], slot, seq).start()
+        relay(step + seqs)
+        slot, seq, side, valid, relayed = chunk(step)
+
+        @pl.when((step == 2 * seqs) & (chip == helper))
+        def _():
+            for which in range(2):
+                share_rows(1, which)
+            for which in range(2):
+                shared_rows(1, which)
+
+        @pl.when(valid)
+        def _():
+            @pl.when(jnp.logical_not(relayed))
+            def _():
+                landed(held.at[slot, seq], t_recv.at[slot, seq])
 
             def add_gradient(role):
                 x = held[slot, seq]
@@ -277,16 +312,17 @@
             roles = 1 + lax.div(chip, helper) * lax.div(KVH - 1 - slot, split) * (last - chip)
             each(roles, add_gradient)
 
-    each(2 * KVH * seqs, work)
+    each((2 * KVH - 1) * seqs, work)
 
     def send_partials(role):
-        def send_partial(unit):
-            for step in range(1, share):
-                lane_to = lax.rem(lane + step, share)
+        def send_partial(step):
+            unit = UNITS - 1 - step
+            for hop in range(1, share):
+                lane_to = lax.rem(lane + hop, share)
                 to(
-                    total.at[role, lane_to * UNITS + unit], partial.at[role, step - 1, unit],
-                    g_send.at[role, step - 1, unit], g_recv.at[role, step - 1, unit],
-                    sibling(step),
+                    total.at[role, lane_to * UNITS + unit], partial.at[role, hop - 1, unit],
+                    g_send.at[role, hop - 1, unit], g_recv.at[role, hop - 1, unit],
+                    sibling(hop),
                 ).start()
 
         each(UNITS, send_partial)
@@ -294,13 +330,14 @@
     def send_sums(role):
         landing = (out, extra)[role]
 
-        def send_sum(unit):
+        def send_sum(step):
+            unit = UNITS - 1 - step
             at = lane * UNITS + unit
             native = native_of((me + role * share) * UNITS + unit)
             device, slot = lax.div(native, UNITS), lax.rem(native, UNITS)
-            for step in range(1, share):
-                landed(partial.at[role, step - 1, unit], g_recv.at[role, step - 1, unit])
-                total[role, at] += partial[role, step - 1, unit]
+            for hop in range(1, share):
+                landed(partial.at[role, hop - 1, unit], g_recv.at[role, hop - 1, unit])
+                total[role, at] += partial[role, hop - 1, unit]
 
             @pl.when(device == me)
             def _():
@@ -375,7 +412,7 @@
         def _():
             landed(held.at[slot, seq], t_send.at[0, slot, seq])
 
-        @pl.when((slot >= chip) & (chip > 0))
+        @pl.when((slot >= chip) & (chip > 0) & (chip < last))
         def _():
             landed(held.at[slot, seq], t_send.at[1, slot, seq])
 

time: 216 us -> 214 us (level)
  the two profiles are of different devices: /device:TPU:1 before, /device:TPU:19 now
where the time goes in v3:
time: 214 us; the launch traced here: 212 us
  Pallas kernels  200 us (93%)
  other arithmetic  11.2 us (5%)
    pallas_call x1, Pallas kernels, gradient_rows(): pl.pallas_call(functools.partial(kernel, n, blocks, seqs), out_shape=jax....  200 us
    sub x1, other arithmetic, per_device(): updated = master - LEARN_RATE * (step_dir + DECAY * master)  6.68 us

profile of v3, /device:TPU:19, one launch (start us, length us, event | category | flops | bytes accessed | tf_op | source)
XLA Modules:
  0.0 212.2 jit_solution(9473651194002569551)
XLA Ops:
  0.7 0.5 fusion.2
  1.2 0.8 pad_maximum_fusion
  2.0 0.0 copy-start.2
  2.0 3.1 %convert_element_type.33 = bf16[1,320,2048]{2,1,0:T(8,128)(2,1)} convert(f32[1,320,2048]{2,1,0:T(8,128)} %param.6) | non-fusion elementwise | flops 655360 | bytes 3932160 | tf_op jit(solution)/shard_map/convert_element_type | solution.py:467
  5.2 0.0 copy-start
  5.2 0.0 copy-start.1
  5.2 200.3 %shard_map.76 = f32[5,64,2048]{2,1,0:T(8,128)} custom-call(bf16[2,256,2048]{2,1,0:T(8,128)(2,1)} %bitcast.12, bf16[5,64,2048]{2,1,0:T(8,128)(2,1)} %bitcast.11, bf16[5,64,2048]{2,1,0:T(8,128)(2,1)} %bitcast.13, f32[256,128]{1,0:T(8,128)} %get-tuple-element.9.cos_ref, f32[256,128]{1,0:T(8,128)} %get-tuple-element.10.sin_ref), custom_call_target="tpu_custom_call" | custom-call | tf_op jit(solution)/shard_map/pallas_call | solution.py:430
  205.5 0.0 copy-done.2
  205.5 0.0 copy-done
  205.5 0.0 copy-done.1
  205.6 6.7 %multiply_subtract_fusion = (f32[1,320,2048]{2,1,0:T(8,128)}, f32[1,320,2048]{2,1,0:T(8,128)}, f32[1,320,2048]{2,1,0:T(8,128)}) fusion(f32[1,320,2048]{2,1,0:T(8,128)S(1)} %copy-done, f32[1,320,2048]{2,1,0:T(8,128)S(1)} %copy-done.1, f32[1,320,2048]{2,1,0:T(8,128)S(1)} %copy-done.2, f32[1,320,2048]{2,1,0:T(8,128)} %bitcast.10), kind=kLoop, calls=%fused_computation.4 | loop fusion | flops 9830400 | bytes 18350080 | tf_op jit(solution)/shard_map/sub | solution.py:475
  (2 shorter events, 0.0 us)
Async XLA Ops:
  2.0 203.5 %copy-start.2 = (f32[1,320,2048]{2,1,0:T(8,128)S(1)}, f32[1,320,2048]{2,1,0:T(8,128)}, u32[]{:S(2)}) copy-start(f32[1,320,2048]{2,1,0:T(8,128)} %param.9) | copy-start | bytes 7864324
  5.2 200.4 %copy-start = (f32[1,320,2048]{2,1,0:T(8,128)S(1)}, f32[1,320,2048]{2,1,0:T(8,128)}, u32[]{:S(2)}) copy-start(f32[1,320,2048]{2,1,0:T(8,128)} %param.6) | copy-start | bytes 7864324
  5.2 200.4 %copy-start.1 = (f32[1,320,2048]{2,1,0:T(8,128)S(1)}, f32[1,320,2048]{2,1,0:T(8,128)}, u32[]{:S(2)}) copy-start(f32[1,320,2048]{2,1,0:T(8,128)} %param.8) | copy-start | bytes 7864324

commit v4 on v3

--- a/solution.py
+++ b/solution.py
@@ -38,13 +38,15 @@
     )
 
 
-def sequence_grad(x, w_student, w_teacher, cosine, sine):
+def group_grad(x, w_student, w_teacher, cosine, sine):
     inv_root = 1.0 / math.sqrt(HD)
 
     def project(weight):
-        raw = lax.dot_general(
+        return lax.dot_general(
             x, weight, (((1,), (1,)), ((), ())), preferred_element_type=jnp.float32
         )
+
+    def heads_of(raw):
         parts = []
         for head in range(GROUP + 1):
             part = raw[:, head * HD : (head + 1) * HD]
@@ -52,7 +54,7 @@
             parts.append(turned.astype(jnp.bfloat16))
         return parts
 
-    student, teacher = project(w_student), project(w_teacher)
+    raw_student, raw_teacher = project(w_student), project(w_teacher)
     rows = lax.broadcasted_iota(jnp.int32, (SEQ, SEQ), 0)
     columns = lax.broadcasted_iota(jnp.int32, (SEQ, SEQ), 1)
     causal = rows >= columns
@@ -71,18 +73,24 @@
     def turn_back(part):
         return (part * cosine - pltpu.roll(part, HD // 2, 1) * sine).astype(jnp.bfloat16)
 
-    pieces = []
-    key_grad = jnp.zeros((SEQ, HD), jnp.float32)
-    for head in range(GROUP):
-        spread = probs(student[head], student[GROUP]) - probs(teacher[head], teacher[GROUP])
-        rounded = (jnp.where(causal, spread, 0.0) * (1.0 / HEADS)).astype(jnp.bfloat16)
-        query_grad = jnp.dot(rounded, student[GROUP], preferred_element_type=jnp.float32)
-        pieces.append(turn_back(query_grad * inv_root))
-        key_grad += lax.dot_general(
-            rounded, student[head], (((0,), (0,)), ((), ())), preferred_element_type=jnp.float32
-        )
-    pieces.append(turn_back(key_grad * inv_root))
-    return jnp.concatenate(pieces, axis=1)
+    results = []
+    for start in range(0, x.shape[0], SEQ):
+        student = heads_of(raw_student[start : start + SEQ])
+        teacher = heads_of(raw_teacher[start : start + SEQ])
+        pieces = []
+        key_grad = jnp.zeros((SEQ, HD), jnp.float32)
+        for head in range(GROUP):
+            spread = probs(student[head], student[GROUP]) - probs(teacher[head], teacher[GROUP])
+            rounded = (jnp.where(causal, spread, 0.0) * (1.0 / HEADS)).astype(jnp.bfloat16)
+            query_grad = jnp.dot(rounded, student[GROUP], preferred_element_type=jnp.float32)
+            pieces.append(turn_back(query_grad * inv_root))
+            key_grad += lax.dot_general(
+                rounded, student[head], (((0,), (0,)), ((), ())),
+                preferred_element_type=jnp.float32,
+            )
+        pieces.append(turn_back(key_grad * inv_root))
+        results.append(jnp.concatenate(pieces, axis=1))
+    return jnp.concatenate(results, axis=0)
 
 
 def kernel(
@@ -248,36 +256,81 @@
     for which in range(2):
         shared_rows(0, which)
 
-    def chunk(step):
-        turn, seq = lax.div(step, seqs), lax.rem(step, seqs)
+    def send_partials(role):
+        def send_partial(step):
+            unit = UNITS - 1 - step
+            for hop in range(1, share):
+                lane_to = lax.rem(lane + hop, share)
+                to(
+                    total.at[role, lane_to * UNITS + unit], partial.at[role, hop - 1, unit],
+                    g_send.at[role, hop - 1, unit], g_recv.at[role, hop - 1, unit],
+                    sibling(hop),
+                ).start()
+
+        each(UNITS, send_partial)
+
+    def send_sums(role):
+        landing = (out, extra)[role]
+
+        def send_sum(step):
+            unit = UNITS - 1 - step
+            at = lane * UNITS + unit
+            native = native_of((me + role * share) * UNITS + unit)
+            device, slot = lax.div(native, UNITS), lax.rem(native, UNITS)
+            for hop in range(1, share):
+                landed(partial.at[role, hop - 1, unit], g_recv.at[role, hop - 1, unit])
+                total[role, at] += partial[role, hop - 1, unit]
+
+            @pl.when(device == me)
+            def _():
+                pltpu.make_async_copy(
+                    total.at[role, at], landing.at[slot], f_recv.at[role, slot]
+                ).start()
+
+            @pl.when(device != me)
+            def _():
+                to(
+                    total.at[role, at], landing.at[slot], f_send.at[role, unit],
+                    f_recv.at[role, slot], device,
+                ).start()
+
+        each(UNITS, send_sum)
+
+    def chunk(turn):
         distance, side = lax.div(turn + 1, 2), lax.rem(turn, 2)
         slot = chip - distance + 2 * distance * side
         valid = (slot >= 0) & (slot < KVH) & ((chip < last) | (slot >= split))
         relayed = valid & (
             ((side == 1) & (chip > 0)) | ((side == 0) & (distance > 0) & (chip < helper))
         )
-        return slot, seq, side, valid, relayed
-
-    def relay(step):
-        slot, seq, side, _, relayed = chunk(step)
+        return slot, side, valid, relayed
+
+    def relay(turn):
+        slot, side, _, relayed = chunk(turn)
+
+        def relay_one(seq):
+            landed(held.at[slot, seq], t_recv.at[slot, seq])
+
+            @pl.when(side == 0)
+            def _():
+                pass_right(held.at[slot, seq], slot, seq).start()
+
+            @pl.when(side == 1)
+            def _():
+                pass_left(held.at[slot, seq], slot, seq).start()
 
         @pl.when(relayed)
         def _():
-            landed(held.at[slot, seq], t_recv.at[slot, seq])
-
-            @pl.when(side == 0)
-            def _():
-                pass_right(held.at[slot, seq], slot, seq).start()
-
-            @pl.when(side == 1)
-            def _():
-                pass_left(held.at[slot, seq], slot, seq).start()
-
-    def work(step):
-        relay(step + seqs)
-        slot, seq, side, valid, relayed = chunk(step)
-
-        @pl.when((step == 2 * seqs) & (chip == helper))
+            each(seqs, relay_one)
+
+    def work(turn):
+        @pl.when(turn >= 2)
+        def _():
+            relay(turn + 1)
+
+        slot, _, valid, relayed = chunk(turn)
+
+        @pl.when((turn == 2) & (chip == helper))
         def _():
             for which in range(2):
                 share_rows(1, which)
@@ -288,11 +341,14 @@
         def _():
             @pl.when(jnp.logical_not(relayed))
             def _():
-                landed(held.at[slot, seq], t_recv.at[slot, seq])
-
-            def add_gradient(role):
-                x = held[slot, seq]
-                grad = sequence_grad(
+                each(seqs, lambda seq: landed(held.at[slot, seq], t_recv.at[slot, seq]))
+
+            roles = 1 + lax.div(chip, helper) * lax.div(KVH - 1 - slot, split) * (last - chip)
+
+            def add_gradient(step):
+                role = roles - 1 - step
+                x = held[slot].reshape(seqs * SEQ, -1)
+                grad = group_grad(
                     x,
                     weight[role, 0].reshape(HEAD_ROWS, -1),
                     weight[role, 1].reshape(HEAD_ROWS, -1),
@@ -309,53 +365,19 @@
                         UNITS * share, -1, width
                     )
 
-            roles = 1 + lax.div(chip, helper) * lax.div(KVH - 1 - slot, split) * (last - chip)
+                @pl.when((role == 1) & (slot == 0))
+                def _():
+                    send_partials(1)
+                    send_sums(1)
+
             each(roles, add_gradient)
 
-    each((2 * KVH - 1) * seqs, work)
-
-    def send_partials(role):
-        def send_partial(step):
-            unit = UNITS - 1 - step
-            for hop in range(1, share):
-                lane_to = lax.rem(lane + hop, share)
-                to(
-                    total.at[role, lane_to * UNITS + unit], partial.at[role, hop - 1, unit],
-                    g_send.at[role, hop - 1, unit], g_recv.at[role, hop - 1, unit],
-                    sibling(hop),
-                ).start()
-
-        each(UNITS, send_partial)
-
-    def send_sums(role):
-        landing = (out, extra)[role]
-
-        def send_sum(step):
-            unit = UNITS - 1 - step
-            at = lane * UNITS + unit
-            native = native_of((me + role * share) * UNITS + unit)
-            device, slot = lax.div(native, UNITS), lax.rem(native, UNITS)
-            for hop in range(1, share):
-                landed(partial.at[role, hop - 1, unit], g_recv.at[role, hop - 1, unit])
-                total[role, at] += partial[role, hop - 1, unit]
-
-            @pl.when(device == me)
-            def _():
-                pltpu.make_async_copy(
-                    total.at[role, at], landing.at[slot], f_recv.at[role, slot]
-                ).start()
-
-            @pl.when(device != me)
-            def _():
-                to(
-                    total.at[role, at], landing.at[slot], f_send.at[role, unit],
-                    f_recv.at[role, slot], device,
-                ).start()
-
-        each(UNITS, send_sum)
-
-    each_role(send_partials)
-    each_role(send_sums)
+    relay(2)
+    relay(1)
+    each(2 * KVH - 1, work)
+
+    send_partials(0)
+    send_sums(0)
 
     def arrive(unit):
         landed(out.at[unit], f_recv.at[0, unit])

time: 214 us -> 212 us (level)
  no operation moved by 1% of the time
where the time goes in v4:
time: 212 us; the launch traced here: 211 us
  Pallas kernels  199 us (94%)
  other arithmetic  11.2 us (5%)
    pallas_call x1, Pallas kernels, gradient_rows(): pl.pallas_call(functools.partial(kernel, n, blocks, seqs), out_shape=jax....  199 us
    sub x1, other arithmetic, per_device(): updated = master - LEARN_RATE * (step_dir + DECAY * master)  6.68 us

profile of v4, /device:TPU:19, one launch (start us, length us, event | category | flops | bytes accessed | tf_op | source)
XLA Modules:
  0.0 211.0 jit_solution(11824263562553354885)
XLA Ops:
  0.7 0.5 fusion.2
  1.2 0.8 pad_maximum_fusion
  2.0 0.0 copy-start.2
  2.0 3.1 %convert_element_type.33 = bf16[1,320,2048]{2,1,0:T(8,128)(2,1)} convert(f32[1,320,2048]{2,1,0:T(8,128)} %param.6) | non-fusion elementwise | flops 655360 | bytes 3932160 | tf_op jit(solution)/shard_map/convert_element_type | solution.py:489
  5.2 0.0 copy-start
  5.2 0.0 copy-start.1
  5.2 199.1 %shard_map.76 = f32[5,64,2048]{2,1,0:T(8,128)} custom-call(bf16[2,256,2048]{2,1,0:T(8,128)(2,1)} %bitcast.12, bf16[5,64,2048]{2,1,0:T(8,128)(2,1)} %bitcast.11, bf16[5,64,2048]{2,1,0:T(8,128)(2,1)} %bitcast.13, f32[256,128]{1,0:T(8,128)} %get-tuple-element.9.cos_ref, f32[256,128]{1,0:T(8,128)} %get-tuple-element.10.sin_ref), custom_call_target="tpu_custom_call" | custom-call | tf_op jit(solution)/shard_map/pallas_call | solution.py:452
  204.3 0.0 copy-done.2
  204.3 0.0 copy-done
  204.3 0.0 copy-done.1
  204.3 6.7 %multiply_subtract_fusion = (f32[1,320,2048]{2,1,0:T(8,128)}, f32[1,320,2048]{2,1,0:T(8,128)}, f32[1,320,2048]{2,1,0:T(8,128)}) fusion(f32[1,320,2048]{2,1,0:T(8,128)S(1)} %copy-done, f32[1,320,2048]{2,1,0:T(8,128)S(1)} %copy-done.1, f32[1,320,2048]{2,1,0:T(8,128)S(1)} %copy-done.2, f32[1,320,2048]{2,1,0:T(8,128)} %bitcast.10), kind=kLoop, calls=%fused_computation.4 | loop fusion | flops 9830400 | bytes 18350080 | tf_op jit(solution)/shard_map/sub | solution.py:497
  (2 shorter events, 0.0 us)
Async XLA Ops:
  2.0 202.2 %copy-start.2 = (f32[1,320,2048]{2,1,0:T(8,128)S(1)}, f32[1,320,2048]{2,1,0:T(8,128)}, u32[]{:S(2)}) copy-start(f32[1,320,2048]{2,1,0:T(8,128)} %param.9) | copy-start | bytes 7864324
  5.2 199.1 %copy-start = (f32[1,320,2048]{2,1,0:T(8,128)S(1)}, f32[1,320,2048]{2,1,0:T(8,128)}, u32[]{:S(2)}) copy-start(f32[1,320,2048]{2,1,0:T(8,128)} %param.6) | copy-start | bytes 7864324
  5.2 199.1 %copy-start.1 = (f32[1,320,2048]{2,1,0:T(8,128)S(1)}, f32[1,320,2048]{2,1,0:T(8,128)}, u32[]{:S(2)}) copy-start(f32[1,320,2048]{2,1,0:T(8,128)} %param.8) | copy-start | bytes 7864324

commit v5 on v4

--- a/solution.py
+++ b/solution.py
@@ -3,6 +3,7 @@
 
 import jax
 import jax.numpy as jnp
+import numpy as np
 from jax import lax
 from jax.experimental import pallas as pl
 from jax.experimental.pallas import tpu as pltpu
@@ -28,13 +29,13 @@
 
 
 def rotary_tables():
-    positions = jnp.arange(SEQ).astype(jnp.float32)
-    exponents = jnp.arange(HD // 2).astype(jnp.float32) * (2.0 / HD)
-    angles = positions[:, None] * (THETA ** (-exponents))[None, :]
-    cosine, sine = jnp.cos(angles), jnp.sin(angles)
+    positions = np.arange(SEQ, dtype=np.float32)
+    exponents = np.arange(HD // 2, dtype=np.float32) * np.float32(2.0 / HD)
+    angles = positions[:, None] * (np.float32(THETA) ** (-exponents))[None, :]
+    cosine, sine = np.cos(angles), np.sin(angles)
     return (
-        jnp.concatenate([cosine, cosine], axis=1),
-        jnp.concatenate([-sine, sine], axis=1),
+        np.concatenate([cosine, cosine], axis=1),
+        np.concatenate([-sine, sine], axis=1),
     )
 
 
@@ -203,15 +204,25 @@
     def pass_left(src, slot, seq):
         return to(src, held.at[slot, seq], t_send.at[1, slot, seq], t_recv.at[slot, seq], me - share)
 
-    for seq in range(seqs):
-
-        @pl.when(chip < KVH - 1)
+    def send_own(seq):
+        @pl.when(chip < last)
         def _():
             pass_right(tokens.at[seq], chip, seq).start()
 
         @pl.when(chip > 0)
         def _():
             pass_left(tokens.at[seq], chip, seq).start()
+
+    def own_left(seq):
+        @pl.when(chip < last)
+        def _():
+            landed(held.at[chip, seq], t_send.at[0, chip, seq])
+
+        @pl.when(chip > 0)
+        def _():
+            landed(held.at[chip, seq], t_send.at[1, chip, seq])
+
+    send_own(0)
 
     total[...] = jnp.zeros_like(total)
 
@@ -245,14 +256,18 @@
         def _():
             body(1)
 
+    for which in range(2):
+        share_rows(0, which)
+
+    for seq in range(1, seqs):
+        own_left(seq - 1)
+        send_own(seq)
+
     @pl.when(chip == last)
     def _():
-        for seq in range(seqs):
-            landed(held.at[chip, seq], t_send.at[1, chip, seq])
+        landed(held.at[chip, seqs - 1], t_send.at[1, chip, seqs - 1])
         each(UNITS, functools.partial(send_rows, role=1))
 
-    for which in range(2):
-        share_rows(0, which)
     for which in range(2):
         shared_rows(0, which)
 
@@ -305,10 +320,11 @@
         )
         return slot, side, valid, relayed
 
-    def relay(turn):
+    def relay(turn, seq):
         slot, side, _, relayed = chunk(turn)
 
-        def relay_one(seq):
+        @pl.when(relayed)
+        def _():
             landed(held.at[slot, seq], t_recv.at[slot, seq])
 
             @pl.when(side == 0)
@@ -319,25 +335,32 @@
             def _():
                 pass_left(held.at[slot, seq], slot, seq).start()
 
-        @pl.when(relayed)
-        def _():
-            each(seqs, relay_one)
+    def add_gradient(role, x):
+        grad = group_grad(
+            x,
+            weight[role, 0].reshape(HEAD_ROWS, -1),
+            weight[role, 1].reshape(HEAD_ROWS, -1),
+            cos_ref[...],
+            sin_ref[...],
+        )
+        width = 512
+        for start in range(0, x.shape[1], width):
+            piece = lax.dot_general(
+                grad, x[:, start : start + width], (((0,), (0,)), ((), ())),
+                preferred_element_type=jnp.float32,
+            )
+            total[role, :, :, start : start + width] += piece.reshape(UNITS * share, -1, width)
+
+    final = 2 * KVH - 3
 
     def work(turn):
         @pl.when(turn >= 2)
         def _():
-            relay(turn + 1)
+            relay(turn + 1, 0)
 
         slot, _, valid, relayed = chunk(turn)
 
-        @pl.when((turn == 2) & (chip == helper))
-        def _():
-            for which in range(2):
-                share_rows(1, which)
-            for which in range(2):
-                shared_rows(1, which)
-
-        @pl.when(valid)
+        @pl.when(valid & (turn < final))
         def _():
             @pl.when(jnp.logical_not(relayed))
             def _():
@@ -345,38 +368,66 @@
 
             roles = 1 + lax.div(chip, helper) * lax.div(KVH - 1 - slot, split) * (last - chip)
 
-            def add_gradient(step):
-                role = roles - 1 - step
-                x = held[slot].reshape(seqs * SEQ, -1)
-                grad = group_grad(
-                    x,
-                    weight[role, 0].reshape(HEAD_ROWS, -1),
-                    weight[role, 1].reshape(HEAD_ROWS, -1),
-                    cos_ref[...],
-                    sin_ref[...],
-                )
-                width = 512
-                for start in range(0, x.shape[1], width):
-                    piece = lax.dot_general(
-                        grad, x[:, start : start + width], (((0,), (0,)), ((), ())),
-                        preferred_element_type=jnp.float32,
-                    )
-                    total[role, :, :, start : start + width] += piece.reshape(
-                        UNITS * share, -1, width
-                    )
+            def run_role(step):
+                role = step + (1 - jnp.minimum(slot, 1)) * (roles - 1 - 2 * step)
+
+                @pl.when((role == 1) & (slot == split - 1))
+                def _():
+                    for which in range(2):
+                        share_rows(1, which)
+                    for which in range(2):
+                        shared_rows(1, which)
+
+                add_gradient(role, held[slot].reshape(seqs * SEQ, -1))
 
                 @pl.when((role == 1) & (slot == 0))
                 def _():
                     send_partials(1)
                     send_sums(1)
 
-            each(roles, add_gradient)
-
-    relay(2)
-    relay(1)
+            each(roles, run_role)
+
+        @pl.when(valid & (turn >= final))
+        def _():
+            def run_sequence(seq):
+                landed(held.at[slot, seq], t_recv.at[slot, seq])
+                add_gradient(0, held[slot, seq])
+
+            each(seqs, run_sequence)
+
+        for seq in range(1, seqs):
+
+            @pl.when(turn >= 2)
+            def _():
+                relay(turn + 1, seq)
+
+            @pl.when(turn == 0)
+            def _():
+                relay(2, seq)
+                relay(1, seq)
+
+    relay(2, 0)
+    relay(1, 0)
     each(2 * KVH - 1, work)
 
+    def sent_tokens(step):
+        slot, seq = lax.div(step, seqs), lax.rem(step, seqs)
+        later = (slot != chip) | (seq == seqs - 1)
+
+        @pl.when(later & (slot <= chip) & ((chip < helper) | ((chip == helper) & (slot == chip))))
+        def _():
+            landed(held.at[slot, seq], t_send.at[0, slot, seq])
+
+        @pl.when(later & (slot >= chip) & (chip > 0) & (chip < last))
+        def _():
+            landed(held.at[slot, seq], t_send.at[1, slot, seq])
+
     send_partials(0)
+
+    @pl.when(lane < share - 1)
+    def _():
+        each(KVH * seqs, sent_tokens)
+
     send_sums(0)
 
     def arrive(unit):
@@ -427,18 +478,9 @@
 
     each_role(shares_left)
 
-    def sent_tokens(step):
-        slot, seq = lax.div(step, seqs), lax.rem(step, seqs)
-
-        @pl.when((slot <= chip) & ((chip < helper) | ((chip == helper) & (slot == chip))))
-        def _():
-            landed(held.at[slot, seq], t_send.at[0, slot, seq])
-
-        @pl.when((slot >= chip) & (chip > 0) & (chip < last))
-        def _():
-            landed(held.at[slot, seq], t_send.at[1, slot, seq])
-
-    each(KVH * seqs, sent_tokens)
+    @pl.when(lane == share - 1)
+    def _():
+        each(KVH * seqs, sent_tokens)
 
 
 def gradient_rows(tokens, student_copy, snapshot, n, blocks):

time: 212 us -> 202 us (0.953)
  Pallas kernels: 199 us -> 190 us
    pallas_call x1, Pallas kernels: 199 us -> 190 us  [gradient_rows(): pl.pallas_call(functools.partial(kernel, n, blocks, seqs), out_shape=jax....]
where the time goes in v5:
time: 202 us; the launch traced here: 200 us
  Pallas kernels  190 us (94%)
  other arithmetic  9.82 us (5%)
    pallas_call x1, Pallas kernels, gradient_rows(): pl.pallas_call(functools.partial(kernel, n, blocks, seqs), out_shape=jax....  190 us
    sub x1, other arithmetic, per_device(): updated = master - LEARN_RATE * (step_dir + DECAY * master)  6.68 us

profile of v5, /device:TPU:19, one launch (start us, length us, event | category | flops | bytes accessed | tf_op | source)
XLA Modules:
  0.0 200.3 jit_solution(18014255146160144098)
XLA Ops:
  0.6 0.0 copy-start.2
  0.6 3.1 %convert_element_type.7 = bf16[1,320,2048]{2,1,0:T(8,128)(2,1)} convert(f32[1,320,2048]{2,1,0:T(8,128)} %param.8) | non-fusion elementwise | flops 655360 | bytes 3932160 | tf_op jit(solution)/shard_map/convert_element_type | solution.py:531
  3.8 0.0 copy-start
  3.8 0.0 copy-start.1
  3.8 189.8 %shard_map.94 = f32[5,64,2048]{2,1,0:T(8,128)} custom-call(bf16[2,256,2048]{2,1,0:T(8,128)(2,1)} %bitcast.12, bf16[5,64,2048]{2,1,0:T(8,128)(2,1)} %bitcast.11, bf16[5,64,2048]{2,1,0:T(8,128)(2,1)} %bitcast.13, f32[256,128]{1,0:T(8,128)} %constant.22.clone.cos_ref, f32[256,128]{1,0:T(8,128)} %constant.23.clone.sin_ref), custom_call_target="tpu_custom_call" | custom-call | tf_op jit(solution)/shard_map/pallas_call | solution.py:494
  193.6 0.0 copy-done.2
  193.6 0.0 copy-done
  193.7 0.0 copy-done.1
  193.7 6.7 %multiply_subtract_fusion = (f32[1,320,2048]{2,1,0:T(8,128)}, f32[1,320,2048]{2,1,0:T(8,128)}, f32[1,320,2048]{2,1,0:T(8,128)}) fusion(f32[1,320,2048]{2,1,0:T(8,128)S(1)} %copy-done, f32[1,320,2048]{2,1,0:T(8,128)S(1)} %copy-done.1, f32[1,320,2048]{2,1,0:T(8,128)S(1)} %copy-done.2, f32[1,320,2048]{2,1,0:T(8,128)} %bitcast.10), kind=kLoop, calls=%fused_computation.4 | loop fusion | flops 9830400 | bytes 18350080 | tf_op jit(solution)/shard_map/sub | solution.py:539
Async XLA Ops:
  0.6 193.0 %copy-start.2 = (f32[1,320,2048]{2,1,0:T(8,128)S(1)}, f32[1,320,2048]{2,1,0:T(8,128)}, u32[]{:S(2)}) copy-start(f32[1,320,2048]{2,1,0:T(8,128)} %param.11) | copy-start | bytes 7864324
  3.8 189.9 %copy-start = (f32[1,320,2048]{2,1,0:T(8,128)S(1)}, f32[1,320,2048]{2,1,0:T(8,128)}, u32[]{:S(2)}) copy-start(f32[1,320,2048]{2,1,0:T(8,128)} %param.8) | copy-start | bytes 7864324
  3.8 189.9 %copy-start.1 = (f32[1,320,2048]{2,1,0:T(8,128)S(1)}, f32[1,320,2048]{2,1,0:T(8,128)}, u32[]{:S(2)}) copy-start(f32[1,320,2048]{2,1,0:T(8,128)} %param.10) | copy-start | bytes 7864324

commit v6 on v5

--- a/solution.py
+++ b/solution.py
@@ -56,20 +56,20 @@
         return parts
 
     raw_student, raw_teacher = project(w_student), project(w_teacher)
-    rows = lax.broadcasted_iota(jnp.int32, (SEQ, SEQ), 0)
-    columns = lax.broadcasted_iota(jnp.int32, (SEQ, SEQ), 1)
-    causal = rows >= columns
-
-    def probs(query, key):
-        scores = (
-            lax.dot_general(
-                query, key, (((1,), (1,)), ((), ())), preferred_element_type=jnp.float32
-            )
-            * inv_root
-        )
-        scores = jnp.where(causal, scores, MASKED)
-        spread = jnp.exp(scores - jnp.max(scores, axis=-1, keepdims=True))
-        return spread * (1.0 / jnp.sum(spread, axis=-1, keepdims=True))
+    half = SEQ // 2
+    base = inv_root * math.log2(math.e)
+
+    def probs(query, key, start):
+        stop = start + half
+        scores = lax.dot_general(
+            query[start:stop], key[:stop], (((1,), (1,)), ((), ())),
+            preferred_element_type=jnp.float32,
+        )
+        rows = lax.broadcasted_iota(jnp.int32, scores.shape, 0) + start
+        columns = lax.broadcasted_iota(jnp.int32, scores.shape, 1)
+        scores = jnp.where(rows >= columns, scores, MASKED)
+        spread = jnp.exp2((scores - jnp.max(scores, axis=-1, keepdims=True)) * base)
+        return spread * (1.0 / (HEADS * jnp.sum(spread, axis=-1, keepdims=True)))
 
     def turn_back(part):
         return (part * cosine - pltpu.roll(part, HD // 2, 1) * sine).astype(jnp.bfloat16)
@@ -81,8 +81,15 @@
         pieces = []
         key_grad = jnp.zeros((SEQ, HD), jnp.float32)
         for head in range(GROUP):
-            spread = probs(student[head], student[GROUP]) - probs(teacher[head], teacher[GROUP])
-            rounded = (jnp.where(causal, spread, 0.0) * (1.0 / HEADS)).astype(jnp.bfloat16)
+            first, second = (
+                (
+                    probs(student[head], student[GROUP], begin)
+                    - probs(teacher[head], teacher[GROUP], begin)
+                ).astype(jnp.bfloat16)
+                for begin in (0, half)
+            )
+            first = jnp.concatenate([first, jnp.zeros_like(first)], axis=1)
+            rounded = jnp.concatenate([first, second], axis=0)
             query_grad = jnp.dot(rounded, student[GROUP], preferred_element_type=jnp.float32)
             pieces.append(turn_back(query_grad * inv_root))
             key_grad += lax.dot_general(
@@ -204,25 +211,19 @@
     def pass_left(src, slot, seq):
         return to(src, held.at[slot, seq], t_send.at[1, slot, seq], t_recv.at[slot, seq], me - share)
 
-    def send_own(seq):
-        @pl.when(chip < last)
-        def _():
-            pass_right(tokens.at[seq], chip, seq).start()
-
-        @pl.when(chip > 0)
-        def _():
-            pass_left(tokens.at[seq], chip, seq).start()
+    right_passes, left_passes = chip < helper - 1, chip > 1
+
+    def own_right(seq):
+        pass_right(tokens.at[seq], chip, seq).start()
 
     def own_left(seq):
-        @pl.when(chip < last)
-        def _():
-            landed(held.at[chip, seq], t_send.at[0, chip, seq])
-
-        @pl.when(chip > 0)
-        def _():
-            landed(held.at[chip, seq], t_send.at[1, chip, seq])
-
-    send_own(0)
+        pass_left(tokens.at[seq], chip, seq).start()
+
+    pl.when(chip < last)(lambda: own_right(0))
+    pl.when(chip > 0)(lambda: own_left(0))
+    for seq in range(1, seqs):
+        pl.when((chip < last) & jnp.logical_not(right_passes))(functools.partial(own_right, seq))
+        pl.when((chip > 0) & jnp.logical_not(left_passes))(functools.partial(own_left, seq))
 
     total[...] = jnp.zeros_like(total)
 
@@ -256,12 +257,20 @@
         def _():
             body(1)
 
+    for seq in range(1, seqs):
+
+        @pl.when(right_passes)
+        def _():
+            landed(held.at[chip, seq - 1], t_send.at[0, chip, seq - 1])
+            own_right(seq)
+
+        @pl.when(left_passes)
+        def _():
+            landed(held.at[chip, seq - 1], t_send.at[1, chip, seq - 1])
+            own_left(seq)
+
     for which in range(2):
         share_rows(0, which)
-
-    for seq in range(1, seqs):
-        own_left(seq - 1)
-        send_own(seq)
 
     @pl.when(chip == last)
     def _():
@@ -414,11 +423,11 @@
         slot, seq = lax.div(step, seqs), lax.rem(step, seqs)
         later = (slot != chip) | (seq == seqs - 1)
 
-        @pl.when(later & (slot <= chip) & ((chip < helper) | ((chip == helper) & (slot == chip))))
+        @pl.when((later | jnp.logical_not(right_passes)) & (slot <= chip) & ((chip < helper) | ((chip == helper) & (slot == chip))))
         def _():
             landed(held.at[slot, seq], t_send.at[0, slot, seq])
 
-        @pl.when(later & (slot >= chip) & (chip > 0) & (chip < last))
+        @pl.when((later | jnp.logical_not(left_passes)) & (slot >= chip) & (chip > 0) & (chip < last))
         def _():
             landed(held.at[slot, seq], t_send.at[1, slot, seq])
 

time: 202 us -> 202 us (level)
  no operation moved by 1% of the time
where the time goes in v6:
time: 202 us; the launch traced here: 201 us
  Pallas kernels  190 us (94%)
  other arithmetic  9.82 us (5%)
    pallas_call x1, Pallas kernels, gradient_rows(): pl.pallas_call(functools.partial(kernel, n, blocks, seqs), out_shape=jax....  190 us
    sub x1, other arithmetic, per_device(): updated = master - LEARN_RATE * (step_dir + DECAY * master)  6.68 us

profile of v6, /device:TPU:19, one launch (start us, length us, event | category | flops | bytes accessed | tf_op | source)
XLA Modules:
  0.0 200.7 jit_solution(17480624690557514293)
XLA Ops:
  0.6 0.0 copy-start.2
  0.6 3.1 %convert_element_type.7 = bf16[1,320,2048]{2,1,0:T(8,128)(2,1)} convert(f32[1,320,2048]{2,1,0:T(8,128)} %param.8) | non-fusion elementwise | flops 655360 | bytes 3932160 | tf_op jit(solution)/shard_map/convert_element_type | solution.py:540
  3.8 0.0 copy-start
  3.8 0.0 copy-start.1
  3.8 190.2 %shard_map.94 = f32[5,64,2048]{2,1,0:T(8,128)} custom-call(bf16[2,256,2048]{2,1,0:T(8,128)(2,1)} %bitcast.12, bf16[5,64,2048]{2,1,0:T(8,128)(2,1)} %bitcast.11, bf16[5,64,2048]{2,1,0:T(8,128)(2,1)} %bitcast.13, f32[256,128]{1,0:T(8,128)} %constant.22.clone.cos_ref, f32[256,128]{1,0:T(8,128)} %constant.23.clone.sin_ref), custom_call_target="tpu_custom_call" | custom-call | tf_op jit(solution)/shard_map/pallas_call | solution.py:503
  194.0 0.0 copy-done.2
  194.0 0.0 copy-done
  194.0 0.0 copy-done.1
  194.0 6.7 %multiply_subtract_fusion = (f32[1,320,2048]{2,1,0:T(8,128)}, f32[1,320,2048]{2,1,0:T(8,128)}, f32[1,320,2048]{2,1,0:T(8,128)}) fusion(f32[1,320,2048]{2,1,0:T(8,128)S(1)} %copy-done, f32[1,320,2048]{2,1,0:T(8,128)S(1)} %copy-done.1, f32[1,320,2048]{2,1,0:T(8,128)S(1)} %copy-done.2, f32[1,320,2048]{2,1,0:T(8,128)} %bitcast.10), kind=kLoop, calls=%fused_computation.4 | loop fusion | flops 9830400 | bytes 18350080 | tf_op jit(solution)/shard_map/sub | solution.py:548
Async XLA Ops:
  0.6 193.3 %copy-start.2 = (f32[1,320,2048]{2,1,0:T(8,128)S(1)}, f32[1,320,2048]{2,1,0:T(8,128)}, u32[]{:S(2)}) copy-start(f32[1,320,2048]{2,1,0:T(8,128)} %param.11) | copy-start | bytes 7864324
  3.8 190.2 %copy-start = (f32[1,320,2048]{2,1,0:T(8,128)S(1)}, f32[1,320,2048]{2,1,0:T(8,128)}, u32[]{:S(2)}) copy-start(f32[1,320,2048]{2,1,0:T(8,128)} %param.8) | copy-start | bytes 7864324
  3.8 190.2 %copy-start.1 = (f32[1,320,2048]{2,1,0:T(8,128)S(1)}, f32[1,320,2048]{2,1,0:T(8,128)}, u32[]{:S(2)}) copy-start(f32[1,320,2048]{2,1,0:T(8,128)} %param.10) | copy-start | bytes 7864324

commit v7 on v6

--- a/solution.py
+++ b/solution.py
@@ -352,10 +352,11 @@
             cos_ref[...],
             sin_ref[...],
         )
+        turned = grad.T
         width = 512
         for start in range(0, x.shape[1], width):
             piece = lax.dot_general(
-                grad, x[:, start : start + width], (((0,), (0,)), ((), ())),
+                turned, x[:, start : start + width], (((1,), (0,)), ((), ())),
                 preferred_element_type=jnp.float32,
             )
             total[role, :, :, start : start + width] += piece.reshape(UNITS * share, -1, width)

time: 202 us -> 202 us (level)
  no operation moved by 1% of the time
where the time goes in v7:
time: 202 us; the launch traced here: 201 us
  Pallas kernels  190 us (94%)
  other arithmetic  9.82 us (5%)
    pallas_call x1, Pallas kernels, gradient_rows(): pl.pallas_call(functools.partial(kernel, n, blocks, seqs), out_shape=jax....  190 us
    sub x1, other arithmetic, per_device(): updated = master - LEARN_RATE * (step_dir + DECAY * master)  6.68 us

profile of v7, /device:TPU:19, one launch (start us, length us, event | category | flops | bytes accessed | tf_op | source)
XLA Modules:
  0.0 200.7 jit_solution(17480624690557514293)
XLA Ops:
  0.6 0.0 copy-start.2
  0.6 3.1 %convert_element_type.7 = bf16[1,320,2048]{2,1,0:T(8,128)(2,1)} convert(f32[1,320,2048]{2,1,0:T(8,128)} %param.8) | non-fusion elementwise | flops 655360 | bytes 3932160 | tf_op jit(solution)/shard_map/convert_element_type | solution.py:541
  3.8 0.0 copy-start
  3.8 0.0 copy-start.1
  3.8 190.2 %shard_map.94 = f32[5,64,2048]{2,1,0:T(8,128)} custom-call(bf16[2,256,2048]{2,1,0:T(8,128)(2,1)} %bitcast.12, bf16[5,64,2048]{2,1,0:T(8,128)(2,1)} %bitcast.11, bf16[5,64,2048]{2,1,0:T(8,128)(2,1)} %bitcast.13, f32[256,128]{1,0:T(8,128)} %constant.22.clone.cos_ref, f32[256,128]{1,0:T(8,128)} %constant.23.clone.sin_ref), custom_call_target="tpu_custom_call" | custom-call | tf_op jit(solution)/shard_map/pallas_call | solution.py:504
  194.0 0.0 copy-done.2
  194.0 0.0 copy-done
  194.0 0.0 copy-done.1
  194.0 6.7 %multiply_subtract_fusion = (f32[1,320,2048]{2,1,0:T(8,128)}, f32[1,320,2048]{2,1,0:T(8,128)}, f32[1,320,2048]{2,1,0:T(8,128)}) fusion(f32[1,320,2048]{2,1,0:T(8,128)S(1)} %copy-done, f32[1,320,2048]{2,1,0:T(8,128)S(1)} %copy-done.1, f32[1,320,2048]{2,1,0:T(8,128)S(1)} %copy-done.2, f32[1,320,2048]{2,1,0:T(8,128)} %bitcast.10), kind=kLoop, calls=%fused_computation.4 | loop fusion | flops 9830400 | bytes 18350080 | tf_op jit(solution)/shard_map/sub | solution.py:549
Async XLA Ops:
  0.6 193.3 %copy-start.2 = (f32[1,320,2048]{2,1,0:T(8,128)S(1)}, f32[1,320,2048]{2,1,0:T(8,128)}, u32[]{:S(2)}) copy-start(f32[1,320,2048]{2,1,0:T(8,128)} %param.11) | copy-start | bytes 7864324
  3.8 190.2 %copy-start = (f32[1,320,2048]{2,1,0:T(8,128)S(1)}, f32[1,320,2048]{2,1,0:T(8,128)}, u32[]{:S(2)}) copy-start(f32[1,320,2048]{2,1,0:T(8,128)} %param.8) | copy-start | bytes 7864324
  3.8 190.2 %copy-start.1 = (f32[1,320,2048]{2,1,0:T(8,128)S(1)}, f32[1,320,2048]{2,1,0:T(8,128)}, u32[]{:S(2)}) copy-start(f32[1,320,2048]{2,1,0:T(8,128)} %param.10) | copy-start | bytes 7864324
